TPU v7x, 256 devices: a whole 4x4x8 slice. The times are simulated.
256 devices in a mesh: leaf: 128 (over z, y_lo, x, core), rhs: 2 (over y_hi).
Axes of the slice: x: 4, y: 4 (y_hi: 2, y_lo: 2; y = y_hi * 2 + y_lo), z: 8, core: 2. Of those that a mesh axis runs over, the one named last changes fastest.
Arguments:
- vectors: bfloat16 [64, 524288], P('rhs', 'leaf'), may hold values from -6 to 6
- leaf_basis: bfloat16 [8192, 64, 64], P('leaf'), may hold values from -0.75 to 0.75
- local_transfer: bfloat16 [16256, 64, 64], P('leaf'), may hold values from -0.5 to 0.5
- coupling: bfloat16 [16256, 4, 64, 64], P('leaf'), may hold values from -0.375 to 0.375
- coupling_source: int32 [16256, 4], P('leaf'), may hold values from 0 to 8191, as said below
- top_transfer: bfloat16 [126, 64, 64], replicated, may hold values from -0.5 to 0.5
- top_coupling: bfloat16 [512, 64, 64], P('leaf'), may hold values from -0.75 to 0.75
- top_target: int32 [512], P('leaf'), may hold values from 2 to 127, as said below
- top_source: int32 [512], P('leaf'), may hold values from 2 to 127, as said below
- near_blocks: bfloat16 [8192, 8, 64, 64], P('leaf', 'rhs'), may hold values from -0.25 to 0.25
- near_source: int32 [8192, 8], P('leaf', 'rhs'), may hold values from 0 to 8191, as said below
Outputs:
- product: bfloat16 [64, 524288], P('rhs', 'leaf')
Inputs may be any that keep to these rules, and one draw needn't show every extreme that they name: `coupling_source`: entry k of a row names a node of that row's level other than the row's own node, at most n away from it along the level, where n is the level's nodes of one subtree; entry 0 is the node's sibling. near_source[t, 0] is t; every other entry of row t lies within 64 leaves of t and differs from t. `top_target`: an upper heap node; top_target[b] and top_source[b] are different nodes of the same upper level. `top_source`: an upper heap node of the same level as top_target[b], never equal to it.
All inputs are finite; a program needn't handle non-finite values.
Results may differ from a plain program's by a relative error of at most 0.025.
Values may be sent and summed in bfloat16 or wider, within the bound.
No kernel may reach another device: no remote copies, remote signals or barrier semaphores. Data moves between devices by JAX's collectives and lax.ppermute only.
A program may use at most 128 MiB of HBM per device.

v0:
```python
import jax
import jax.numpy as jnp
from jax import lax
from jax.sharding import PartitionSpec as P

full_precision = lax.Precision.HIGHEST


def padded(array, sides, width):
    for axis, dim in sides:
        size, length = (lax.axis_size(axis), array.shape[dim])
        up = [(i, (i + 1) % size) for i in range(size - 1)]
        down = [(j, i) for i, j in up]
        last = lax.slice_in_dim(array, length - width, length, axis=dim)
        initial = lax.slice_in_dim(array, 0, width, axis=dim)
        before = lax.ppermute(last, axis, up)
        after = lax.ppermute(initial, axis, down)
        array = jnp.concatenate([before, array, after], axis=dim)
    return array


def level_table(leaf_count):
    layout = []
    first_node = 0
    node_count = leaf_count
    while node_count >= 1:
        layout.append((first_node, node_count))
        first_node += node_count
        node_count //= 2
    return layout


def descend(upper_field, top_transfer, root_count):
    upper_down = upper_field[:, 2:4]
    level_size = 4
    while level_size < root_count:
        parents = jnp.repeat(upper_down, 2, axis=1)
        transfer_rows = top_transfer[level_size - 2 : 2 * level_size - 2].astype(jnp.float32)
        upper_down = upper_field[:, level_size : 2 * level_size] + jnp.einsum(
            "rhb,hab->rha", parents, transfer_rows, precision=full_precision
        )
        level_size *= 2
    return upper_down


def shards(
    vectors,
    leaf_basis,
    local_transfer,
    coupling,
    coupling_source,
    top_transfer,
    top_coupling,
    top_target,
    top_source,
    near_blocks,
    near_source,
):
    rhs_local = vectors.shape[0]
    leaf_count = leaf_basis.shape[0]
    leaf_size = leaf_basis.shape[1]
    rank_size = leaf_basis.shape[2]
    slot_count = coupling.shape[1]
    node_total = coupling.shape[0]
    layout = level_table(leaf_count)
    root_count = lax.axis_size("leaf")
    my_index = lax.axis_index("leaf")
    leaf_points = vectors.reshape(rhs_local, leaf_count, leaf_size)
    coefficients = [
        jnp.einsum(
            "rip,ipk->rik", leaf_points, leaf_basis, preferred_element_type=jnp.float32
        ).astype(jnp.bfloat16)
    ]
    for height in range(1, len(layout)):
        first_node, node_count = layout[height - 1]
        lifted = jnp.einsum(
            "rik,ikm->rim",
            coefficients[-1],
            local_transfer[first_node : first_node + node_count],
            preferred_element_type=jnp.float32,
        )
        coefficients.append(
            lifted.reshape(rhs_local, node_count // 2, 2, rank_size)
            .sum(axis=2)
            .astype(jnp.bfloat16)
        )
    fields = []
    for height in range(len(layout)):
        node_count = layout[height][1]
        extended = padded(coefficients[height], (("leaf", 1),), node_count)
        couple_first_node, couple_node_count = layout[height]
        source_ids = (
            coupling_source[couple_first_node : couple_first_node + couple_node_count]
            - (my_index - 1) * couple_node_count
        )
        picked = jnp.take(extended, source_ids.reshape(-1), axis=1).reshape(
            rhs_local, couple_node_count, slot_count, rank_size
        )
        fields.append(
            jnp.einsum(
                "rtkm,tkmn->rtn",
                picked,
                coupling[couple_first_node : couple_first_node + couple_node_count],
                preferred_element_type=jnp.float32,
            )
        )
    root_row = node_total - 1
    root_transfer = local_transfer[root_row : root_row + 1]
    root_term = jnp.einsum(
        "rdk,dkm->rdm", coefficients[-1], root_transfer, preferred_element_type=jnp.float32
    )
    root_terms = lax.all_gather(root_term, "leaf", axis=1, tiled=True)
    upper = [
        root_terms.reshape(rhs_local, root_count // 2, 2, rank_size)
        .sum(axis=2)
        .astype(jnp.bfloat16)
    ]
    level_size = root_count // 2
    while level_size > 2:
        lifted = jnp.einsum(
            "rhk,hkm->rhm",
            upper[0],
            top_transfer[level_size - 2 : 2 * level_size - 2],
            preferred_element_type=jnp.float32,
        )
        upper.insert(
            0,
            lifted.reshape(rhs_local, level_size // 2, 2, rank_size)
            .sum(axis=2)
            .astype(jnp.bfloat16),
        )
        level_size //= 2
    heap_coef = jnp.concatenate(
        [jnp.zeros((rhs_local, 2, rank_size), jnp.bfloat16)] + upper, axis=1
    )
    sources_up = jnp.take(heap_coef, top_source, axis=1)
    contrib = jnp.einsum(
        "rbm,bmn->rbn", sources_up, top_coupling, preferred_element_type=jnp.float32
    )
    onehot_targets = (
        top_target[:, None] == jnp.arange(root_count, dtype=jnp.int32)[None, :]
    ).astype(jnp.float32)
    partial_field = jnp.einsum("rbn,bh->rhn", contrib, onehot_targets, precision=full_precision)
    upper_field = lax.psum(partial_field, "leaf")
    upper_down = descend(upper_field, top_transfer, root_count)
    parent_down = lax.dynamic_slice_in_dim(upper_down, my_index // 2, 1, axis=1)
    descent = (
        fields[-1]
        + jnp.einsum(
            "rdb,dab->rda", parent_down, root_transfer.astype(jnp.float32), precision=full_precision
        )
    ).astype(jnp.bfloat16)
    for height in range(len(layout) - 2, -1, -1):
        first_node, node_count = layout[height]
        parents = jnp.repeat(descent, 2, axis=1)
        descent = (
            fields[height]
            + jnp.einsum(
                "rtb,tab->rta",
                parents,
                local_transfer[first_node : first_node + node_count],
                preferred_element_type=jnp.float32,
            )
        ).astype(jnp.bfloat16)
    far_part = jnp.einsum("rik,ipk->rip", descent, leaf_basis, preferred_element_type=jnp.float32)
    all_columns = lax.all_gather(vectors, "rhs", axis=0, tiled=True)
    points = padded(all_columns, (("leaf", 1),), vectors.shape[1])
    leaves_seen = points.reshape(points.shape[0], -1, leaf_size)
    positions = near_source - (my_index - 1) * leaf_count
    gathered = jnp.take(leaves_seen, positions.reshape(-1), axis=1).reshape(
        points.shape[0], leaf_count, near_source.shape[1], leaf_size
    )
    near_sum = lax.psum_scatter(
        jnp.einsum("rijq,ijpq->rip", gathered, near_blocks, preferred_element_type=jnp.float32),
        "rhs",
        scatter_dimension=0,
        tiled=True,
    )
    return (far_part + near_sum).reshape(rhs_local, -1).astype(jnp.bfloat16)


def solution(mesh):
    placed = (
        P("rhs", "leaf"),
        P("leaf", None, None),
        P("leaf", None, None),
        P("leaf", None, None, None),
        P("leaf", None),
        P(),
        P("leaf", None, None),
        P("leaf"),
        P("leaf"),
        P("leaf", "rhs", None, None),
        P("leaf", "rhs"),
    )
    return jax.shard_map(
        shards, mesh=mesh, in_specs=placed, out_specs=P("rhs", "leaf"), check_vma=False
    )
```

profile of v0, /device:TPU:1, one launch (start us, length us, event | category | flops | bytes accessed | tf_op | source)
XLA Modules:
  0.0 1447.1 jit_solution(16720337672060827694)
XLA Ops:
  19.8 3.2 copy.156
  37.7 4.5 collective-permute-start.12
  44.7 3.1 collective-permute-start.10
  49.7 3.6 collective-permute-start.8
  75.8 12.2 all_gather.7
  95.6 5.8 slice.126
  101.4 3.2 slice.123
  104.6 3.2 slice.120
  107.8 3.2 slice.117
  111.1 3.3 slice.114
  114.3 3.2 slice.111
  128.7 4.6 copy.165
  134.0 4.7 copy.163
  139.3 4.9 copy.161
  144.8 4.6 copy.159
  150.1 5.0 copy.157
  155.8 6.1 copy.155
  163.3 7.3 copy.153
  172.8 3.3 collective-permute-start.6
  183.2 3.6 collective-permute-start.4
  194.1 3.6 collective-permute-start.2
  205.3 3.6 collective-permute-start
  217.0 3.6 collective-permute-start.14
  231.7 2.9 gather_fusion.1
  237.3 3.7 gather_fusion
  241.0 39.0 %all-gather.2.cloned.1.call-done = f32[32,128,64]{2,0,1:T(8,128)} async-done(((f32[32,1,64]{2,0,1:T(8,128)}), f32[32,128,64]{2,0,1:T(8,128)}) %all-gather.2.cloned.1.call-update) | async-done | bytes 1048592 | tf_op jit(solution)/shard_map/all_gather | solution.py:112
  295.5 5.7 reshape.461
  301.2 5.6 copy.144
  306.8 5.2 gather_fusion.8
  311.9 6.2 fusion.7
  318.1 1056.5 %all-reduce.2.cloned.1.call-done = f32[32,128,64]{1,2,0:T(8,128)} async-done(((f32[32,128,64]{1,2,0:T(8,128)}), f32[32,128,64]{1,2,0:T(8,128)}) %all-reduce.2.cloned.1.call-update) | async-done | bytes 1048592 | tf_op jit(solution)/shard_map/psum | solution.py:144
  1431.5 5.3 fusion.20
  (272 shorter events, 197.3 us)
Async XLA Ops:
  7.4 23.8 %copy-start = (bf16[64,64,64]{2,1,0:T(8,128)(2,1)S(1)}, bf16[64,64,64]{2,1,0:T(8,128)(2,1)}, u32[]{:S(2)}) copy-start(bf16[64,64,64]{2,1,0:T(8,128)(2,1)} %param.12) | copy-start | bytes 1572868
  7.4 272.7 %all-gather.2.cloned.1.call-start = ((), (), s32[]{:S(2)}) async-start(), calls=%async_computation.1 | async-start | bytes 2113536 | tf_op jit(solution)/shard_map/all_gather | solution.py:112
  19.8 12.9 copy-start.5
  33.2 55.4 %copy-start.4 = (bf16[126,64,64]{0,2,1:T(8,128)(2,1)S(1)}, bf16[126,64,64]{0,2,1:T(8,128)(2,1)}, u32[]{:S(2)}) copy-start(bf16[126,64,64]{0,2,1:T(8,128)(2,1)} %param.16) | copy-start | bytes 3096580
  37.7 132.9 %collective-permute-start.12 = (bf16[32,1,64]{2,0,1:T(8,128)(2,1)}, bf16[32,1,64]{2,0,1:T(8,128)(2,1)}, u32[]{:S(2)}, u32[]{:S(2)}) collective-permute-start(bf16[32,1,64]{2,0,1:T(8,128)(2,1)} %bitcast.60), channel_id=1, source_target_pairs={{0,2},{2,4},{4,6},{6,8},{8,10},{10,12},{12,14},{14,16},{16,18},{18... | collective-permute-start | bytes 12296 | tf_op jit(solution)/shard_map/ppermute | solution.py:16
  42.2 130.7 %collective-permute-start.13 = (bf16[32,1,64]{2,0,1:T(8,128)(2,1)}, bf16[32,1,64]{2,0,1:T(8,128)(2,1)}, u32[]{:S(2)}, u32[]{:S(2)}) collective-permute-start(bf16[32,1,64]{2,0,1:T(8,128)(2,1)} %bitcast.60), channel_id=1, source_target_pairs={{2,0},{4,2},{6,4},{8,6},{10,8},{12,10},{14,12},{16,14},{18,16},{20... | collective-permute-start | bytes 12296 | tf_op jit(solution)/shard_map/ppermute | solution.py:17
  44.7 136.6 %collective-permute-start.10 = (bf16[32,2,64]{2,0,1:T(8,128)(2,1)}, bf16[32,2,64]{2,0,1:T(8,128)(2,1)}, u32[]{:S(2)}, u32[]{:S(2)}) collective-permute-start(bf16[32,2,64]{2,0,1:T(8,128)(2,1)} %bitcast_reduce_fusion.10), channel_id=1, source_target_pairs={{0,2},{2,4},{4,6},{6,8},{8,10},{10,12},{12,14},{14,16},{16,18},{18... | collective-permute-start | bytes 24584 | tf_op jit(solution)/shard_map/ppermute | solution.py:16
  47.7 135.4 %collective-permute-start.11 = (bf16[32,2,64]{2,0,1:T(8,128)(2,1)}, bf16[32,2,64]{2,0,1:T(8,128)(2,1)}, u32[]{:S(2)}, u32[]{:S(2)}) collective-permute-start(bf16[32,2,64]{2,0,1:T(8,128)(2,1)} %bitcast_reduce_fusion.10), channel_id=1, source_target_pairs={{2,0},{4,2},{6,4},{8,6},{10,8},{12,10},{14,12},{16,14},{18,16},{20... | collective-permute-start | bytes 24584 | tf_op jit(solution)/shard_map/ppermute | solution.py:17
  49.7 142.5 %collective-permute-start.8 = (bf16[32,4,64]{2,0,1:T(8,128)(2,1)}, bf16[32,4,64]{2,0,1:T(8,128)(2,1)}, u32[]{:S(2)}, u32[]{:S(2)}) collective-permute-start(bf16[32,4,64]{2,0,1:T(8,128)(2,1)} %bitcast_reduce_fusion.8), channel_id=1, source_target_pairs={{0,2},{2,4},{4,6},{6,8},{8,10},{10,12},{12,14},{14,16},{16,18},{18... | collective-permute-start | bytes 49160 | tf_op jit(solution)/shard_map/ppermute | solution.py:16
  57.8 1316.8 %all-reduce.2.cloned.1.call-start = ((), (), s32[]{:S(2)}) async-start(), calls=%async_computation.2 | async-start | bytes 2097152 | tf_op jit(solution)/shard_map/psum | solution.py:144
  95.6 5.8 copy-start.1
  121.5 160.9 %copy-start.9 = (bf16[32,64,64]{2,1,0:T(8,128)(2,1)}, bf16[32,64,64]{2,1,0:T(8,128)(2,1)S(1)}, u32[]{:S(2)}) copy-start(bf16[32,64,64]{2,1,0:T(8,128)(2,1)S(1)} %copy.168) | copy-start | bytes 786436
  124.1 9.3 copy-start.40
  138.7 5.5 copy-start.42
  149.4 5.7 copy-start.37
  155.8 6.1 copy-start.39
  155.8 6.8 copy-start.38
  163.3 42.0 %copy-start.13 = (bf16[32,64,64]{2,0,1:T(8,128)(2,1)S(1)}, bf16[32,64,64]{2,0,1:T(8,128)(2,1)}, u32[]{:S(2)}) copy-start(bf16[32,64,64]{2,0,1:T(8,128)(2,1)} %copy-done.12) | copy-start | bytes 786436
  170.6 23.5 %collective-permute-start.9 = (bf16[32,4,64]{2,0,1:T(8,128)(2,1)}, bf16[32,4,64]{2,0,1:T(8,128)(2,1)}, u32[]{:S(2)}, u32[]{:S(2)}) collective-permute-start(bf16[32,4,64]{2,0,1:T(8,128)(2,1)} %bitcast_reduce_fusion.8), channel_id=1, source_target_pairs={{2,0},{4,2},{6,4},{8,6},{10,8},{12,10},{14,12},{16,14},{18,16},{20... | collective-permute-start | bytes 49160 | tf_op jit(solution)/shard_map/ppermute | solution.py:17
  172.8 30.5 %collective-permute-start.6 = (bf16[32,8,64]{2,0,1:T(8,128)(2,1)}, bf16[32,8,64]{2,0,1:T(8,128)(2,1)}, u32[]{:S(2)}, u32[]{:S(2)}) collective-permute-start(bf16[32,8,64]{2,0,1:T(8,128)(2,1)} %copy-done.26), channel_id=1, source_target_pairs={{0,2},{2,4},{4,6},{6,8},{8,10},{10,12},{12,14},{14,16},{16,18},{18... | collective-permute-start | bytes 98312 | tf_op jit(solution)/shard_map/ppermute | solution.py:16
  181.3 24.0 %collective-permute-start.7 = (bf16[32,8,64]{2,0,1:T(8,128)(2,1)}, bf16[32,8,64]{2,0,1:T(8,128)(2,1)}, u32[]{:S(2)}, u32[]{:S(2)}) collective-permute-start(bf16[32,8,64]{2,0,1:T(8,128)(2,1)} %copy-done.26), channel_id=1, source_target_pairs={{2,0},{4,2},{6,4},{8,6},{10,8},{12,10},{14,12},{16,14},{18,16},{20... | collective-permute-start | bytes 98312 | tf_op jit(solution)/shard_map/ppermute | solution.py:17
  183.2 31.9 %collective-permute-start.4 = (bf16[32,16,64]{2,0,1:T(8,128)(2,1)}, bf16[32,16,64]{2,0,1:T(8,128)(2,1)}, u32[]{:S(2)}, u32[]{:S(2)}) collective-permute-start(bf16[32,16,64]{2,0,1:T(8,128)(2,1)} %copy-done.20), channel_id=1, source_target_pairs={{0,2},{2,4},{4,6},{6,8},{8,10},{10,12},{12,14},{14,16},{16,18},{18... | collective-permute-start | bytes 196616 | tf_op jit(solution)/shard_map/ppermute | solution.py:16
  192.1 24.8 %collective-permute-start.5 = (bf16[32,16,64]{2,0,1:T(8,128)(2,1)}, bf16[32,16,64]{2,0,1:T(8,128)(2,1)}, u32[]{:S(2)}, u32[]{:S(2)}) collective-permute-start(bf16[32,16,64]{2,0,1:T(8,128)(2,1)} %copy-done.20), channel_id=1, source_target_pairs={{2,0},{4,2},{6,4},{8,6},{10,8},{12,10},{14,12},{16,14},{18,16},{20... | collective-permute-start | bytes 196616 | tf_op jit(solution)/shard_map/ppermute | solution.py:17
  194.1 33.5 %collective-permute-start.2 = (bf16[32,32,64]{2,0,1:T(8,128)(2,1)}, bf16[32,32,64]{2,0,1:T(8,128)(2,1)}, u32[]{:S(2)}, u32[]{:S(2)}) collective-permute-start(bf16[32,32,64]{2,0,1:T(8,128)(2,1)} %copy-done.17), channel_id=1, source_target_pairs={{0,2},{2,4},{4,6},{6,8},{8,10},{10,12},{12,14},{14,16},{16,18},{18... | collective-permute-start | bytes 393224 | tf_op jit(solution)/shard_map/ppermute | solution.py:16
  203.3 26.2 %collective-permute-start.3 = (bf16[32,32,64]{2,0,1:T(8,128)(2,1)}, bf16[32,32,64]{2,0,1:T(8,128)(2,1)}, u32[]{:S(2)}, u32[]{:S(2)}) collective-permute-start(bf16[32,32,64]{2,0,1:T(8,128)(2,1)} %copy-done.17), channel_id=1, source_target_pairs={{2,0},{4,2},{6,4},{8,6},{10,8},{12,10},{14,12},{16,14},{18,16},{20... | collective-permute-start | bytes 393224 | tf_op jit(solution)/shard_map/ppermute | solution.py:17
  205.3 29.3 %collective-permute-start = (bf16[32,64,64]{2,0,1:T(8,128)(2,1)S(1)}, bf16[32,64,64]{2,0,1:T(8,128)(2,1)}, u32[]{:S(2)}, u32[]{:S(2)}) collective-permute-start(bf16[32,64,64]{2,0,1:T(8,128)(2,1)S(1)} %copy-done.13), channel_id=1, source_target_pairs={{0,2},{2,4},{4,6},{6,8},{8,10},{10,12},{12,14},{14,16},{16,18},{18... | collective-permute-start | bytes 786440 | tf_op jit(solution)/shard_map/ppermute | solution.py:16
  215.0 19.6 %collective-permute-start.1 = (bf16[32,64,64]{2,0,1:T(8,128)(2,1)S(1)}, bf16[32,64,64]{2,0,1:T(8,128)(2,1)}, u32[]{:S(2)}, u32[]{:S(2)}) collective-permute-start(bf16[32,64,64]{2,0,1:T(8,128)(2,1)S(1)} %copy-done.13), channel_id=1, source_target_pairs={{2,0},{4,2},{6,4},{8,6},{10,8},{12,10},{14,12},{16,14},{18,16},{20... | collective-permute-start | bytes 786440 | tf_op jit(solution)/shard_map/ppermute | solution.py:17
  217.0 76.0 %collective-permute-start.14 = (bf16[64,4096]{1,0:T(8,128)(2,1)}, bf16[64,4096]{1,0:T(8,128)(2,1)}, u32[]{:S(2)}, u32[]{:S(2)}) collective-permute-start(bf16[64,4096]{1,0:T(8,128)(2,1)} %all_gather.7), channel_id=1, source_target_pairs={{0,2},{2,4},{4,6},{6,8},{8,10},{10,12},{12,14},{14,16},{16,18},{18... | collective-permute-start | bytes 1572872 | tf_op jit(solution)/shard_map/ppermute | solution.py:16
  227.6 65.4 %collective-permute-start.15 = (bf16[64,4096]{1,0:T(8,128)(2,1)}, bf16[64,4096]{1,0:T(8,128)(2,1)}, u32[]{:S(2)}, u32[]{:S(2)}) collective-permute-start(bf16[64,4096]{1,0:T(8,128)(2,1)} %all_gather.7), channel_id=1, source_target_pairs={{2,0},{4,2},{6,4},{8,6},{10,8},{12,10},{14,12},{16,14},{18,16},{20... | collective-permute-start | bytes 1572872 | tf_op jit(solution)/shard_map/ppermute | solution.py:17
  282.7 10.3 copy-start.18
  292.9 1138.6 %reduce-scatter.2.cloned.1.call-start = ((), (), s32[]{:S(2)}) async-start(), calls=%async_computation.3 | async-start | bytes 3145728 | tf_op jit(solution)/shard_map/reduce_scatter | solution.py:173
  1374.6 9.6 copy-start.3
  (30 other events, 82.2 us)
Sparse Core Ops, SparseCore 0:
  58.0 222.0 all-gather.1
  293.0 1081.5 all-reduce.1
Sparse Core Ops, SparseCore 1:
  318.2 39.5 reduce-scatter.1
where the time goes:
time: 1460 us; the launch traced here: 1450 us
  waiting for transfers between devices  1100 us (75%)
  local copies, waits for them, and re-layouts  184 us (13%)
  matrix products  49 us (3%)
  starting transfers between devices  45.4 us (3%)
  other arithmetic  45 us (3%)
  between operations  16.1 us (1%)
    psum x1, waiting for transfers between devices, shards(): upper_field = lax.psum(partial_field, 'leaf')  1060 us
    unnamed x111, local copies, waits for them, and re-layouts  67.1 us
    all_gather x1, waiting for transfers between devices, shards(): root_terms = lax.all_gather(root_term, 'leaf', axis=1, tiled=True)  39 us
  transfers between devices with their start and end apart: 19, of which 2 were waited for; matrix products, arithmetic and copies ran while one was open for 17% of the time, Pallas kernels for 0%

commit v1 on v0

v1 whole, which is shorter than its diff:
```python
import functools

import jax
import jax.numpy as jnp
import numpy as np
from jax import lax
from jax.experimental import pallas as pl
from jax.experimental.pallas import tpu as pltpu
from jax.sharding import PartitionSpec as P

BF = jnp.bfloat16
F32 = jnp.float32
VMEM_LIMIT = 44 * 1024 * 1024

NODES = 128
SIZES = (64, 32, 16, 8, 4, 2, 1)
FIRST = (0, 64, 96, 112, 120, 124, 126)
SLOT = (0, 32, 48, 56, 60, 62, 63)
R = 32


def _nn(a, b):
    return lax.dot_general(a, b, (((1,), (0,)), ((), ())), preferred_element_type=F32)


def _nt(a, b):
    return lax.dot_general(a, b, (((1,), (1,)), ((), ())), preferred_element_type=F32)


def _low(rows):
    return lax.broadcasted_iota(jnp.int32, (rows, 128), 1) < 64


def _eye(lanes):
    row = lax.broadcasted_iota(jnp.int32, (128, lanes), 0)
    col = lax.broadcasted_iota(jnp.int32, (128, lanes), 1)
    return jnp.where(row == col, 1.0, 0.0).astype(BF)


def _pick_half(low, half, x, zero):
    return jnp.where(low == (half == 0), x, zero)


def _roll(x):
    return pltpu.roll(x, 64, 1)


def _unstack(raw_ref, wide, count):
    eye = _eye(raw_ref.shape[2])

    def body(k, carry):
        block = raw_ref[k]
        both = jnp.concatenate([block, block], axis=0)
        wide[pl.ds(k, NODES, stride=64), :] = _nt(eye, both)
        return carry

    lax.fori_loop(0, count, body, 0, unroll=8)


def up_kernel(v_ref, basis_ref, raw_ref, msg_ref, root_ref, wide_ref, wide):
    _unstack(raw_ref, wide, 64)

    def narrow(i, carry):
        rows = pl.ds(pl.multiple_of(i * 512, 512), 512)
        wide_ref[rows, :] = wide[rows, :].astype(BF)
        return carry

    lax.fori_loop(0, 16, narrow, 0, unroll=2)
    low = _low(R)
    zero = jnp.zeros((R, 128), BF)
    for p in range(32):
        v = v_ref[:, 128 * p : 128 * p + 128]
        msg_ref[64 + p] = v
        both = jnp.concatenate([jnp.where(low, v, zero), jnp.where(low, zero, v)], axis=0)
        y = _nn(both, basis_ref[2 * p : 2 * p + 2].reshape(128, 64))
        msg_ref[p] = jnp.concatenate([y[:R], y[R:]], axis=1).astype(BF)
    for level in range(1, 7):
        for s in range(max(1, SIZES[level] // 2)):
            parts = []
            for q in (2 * s, 2 * s + 1)[: min(2, SIZES[level])]:
                row = (FIRST[level - 1] + 2 * q) * 64
                parts.append(_nn(msg_ref[SLOT[level - 1] + q], wide_ref[row : row + 128, :]))
            value = parts[0] if len(parts) == 1 else jnp.where(low, parts[0], parts[1])
            msg_ref[SLOT[level] + s] = value.astype(BF)
    root_ref[...] = _nn(msg_ref[63][:, :64], wide_ref[126 * 64 : 127 * 64, :])


def pack_kernel(core_ref, mine_ref, other_ref, out_ref):
    core = core_ref[0]
    total = mine_ref[...] + other_ref[...]
    half = jnp.where(core == 0, total[:16], total[16:])
    packed = jnp.where(_low(8), half[:8], half[8:]).astype(BF)
    out_ref[...] = jnp.broadcast_to(packed[None], out_ref.shape)


def upper_kernel(ids_ref, ids2_ref, gathered_ref, raw_ref, blocks_ref, blocks2_ref, out_ref, wide, coef, field):
    _unstack(raw_ref, wide, 64)
    low8, low = _low(8), _low(16)
    zero = jnp.zeros((16, 128), BF)
    zero32 = jnp.zeros((16, 128), F32)
    for s in range(32):
        a, b = gathered_ref[2 * s].astype(F32), gathered_ref[2 * s + 1].astype(F32)
        top = jnp.where(low8, a, _roll(b))
        bottom = jnp.where(low8, _roll(a), b)
        coef[32 + s] = jnp.concatenate([top, bottom], axis=0).astype(BF)
    field[...] = jnp.zeros_like(field)
    size = 32
    while size >= 2:
        for s in range(size // 2, size):
            parts = []
            for h in (2 * s, 2 * s + 1):
                row = (2 * h - 2) * 64
                parts.append(_nn(coef[h], wide[row : row + 128, :].astype(BF)))
            coef[s] = jnp.where(low, parts[0], parts[1]).astype(BF)
        size //= 2
    for b in range(8):
        ids, blocks, k = (ids_ref, blocks_ref, b) if b < 4 else (ids2_ref, blocks2_ref, b - 4)
        target, source = ids[k], ids[4 + k]
        block = blocks[k]
        block = jnp.concatenate([block, block], axis=0)
        block = jnp.concatenate([block, block], axis=1)
        x = _pick_half(low, source % 2, coef[source // 2], zero)
        field[target // 2] += _pick_half(low, target % 2, _nn(x, block), zero32)
    for h in range(2, 64):
        row = (2 * h - 2) * 64
        x = _pick_half(low, h % 2, field[h // 2].astype(BF), zero)
        field[h] += _nt(x, wide[row : row + 128, :].astype(BF))
    for s in range(32):
        x = field[32 + s]
        top, bottom = x[:8], x[8:]
        out_ref[2 * s] = jnp.where(low8, top, _roll(bottom)).astype(BF)
        out_ref[2 * s + 1] = jnp.where(low8, _roll(top), bottom).astype(BF)


def near_kernel(ids_ref, left_ref, own_ref, right_ref, other_ref, blocks_ref, mine_out, other_out, leaves):
    step = pl.program_id(0)

    @pl.when(step == 0)
    def _():
        for part, ref in enumerate((left_ref, own_ref, right_ref)):

            def body(s, carry, ref=ref, part=part):
                x, y = ref[64 + s], other_ref[32 * part + s]
                z = jnp.concatenate([x, y], axis=0)
                e = 64 * part + 2 * s
                leaves[e] = z[:, :64]
                leaves[e + 1] = z[:, 64:]
                return carry

            lax.fori_loop(0, 32, body, 0, unroll=4)

    for p in range(4):
        parts = []
        for i in (2 * p, 2 * p + 1):
            leaf = step * 8 + i
            total = _nt(leaves[ids_ref[0, leaf]], blocks_ref[i, 0])
            for j in range(1, 4):
                total += _nt(leaves[ids_ref[j, leaf]], blocks_ref[i, j])
            parts.append(total)
        pair = jnp.concatenate(parts, axis=1)
        mine_out[:, 128 * p : 128 * p + 128] = pair[:R]
        other_out[:, 128 * p : 128 * p + 128] = pair[R:].astype(BF)


CHUNK = 8


def field_kernel(ids_ref, left_ref, own_ref, right_ref, raw_ref, out_ref, wide, coef):
    step = pl.program_id(0)
    eye = _eye(raw_ref.shape[3])
    low = _low(R)
    for k in range(2):

        def body(m, carry, k=k):
            both = jnp.concatenate([raw_ref[k, m], raw_ref[k + 2, m]], axis=0)
            row = k * 64 + step * CHUNK + m
            wide[pl.ds(row, NODES, stride=128), :] = _nt(eye, both)
            return carry

        lax.fori_loop(0, CHUNK, body, 0, unroll=True)

    @pl.when(step == 64 // CHUNK - 1)
    def _():
        for part, ref in enumerate((left_ref, own_ref, right_ref)):

            def spread(s, carry, ref=ref, part=part):
                x = ref[s]
                y = jnp.concatenate([x[:, 64:], x[:, :64]], axis=1)
                coef[part * NODES + 2 * s] = jnp.where(low, x, y)
                coef[part * NODES + 2 * s + 1] = jnp.where(low, y, x)
                return carry

            lax.fori_loop(0, 64, spread, 0, unroll=4)

        def node(t):
            a = jnp.where(low, coef[ids_ref[0, t]], coef[ids_ref[1, t]])
            b = jnp.where(low, coef[ids_ref[2, t]], coef[ids_ref[3, t]])
            rows = pl.ds(pl.multiple_of(t * 128, 128), 128)
            y = _nn(jnp.concatenate([a, b], axis=0), wide[rows, :].astype(BF))
            return y[:R], y[R:]

        def pair(s, carry):
            a0, b0 = node(2 * s)
            a1, b1 = node(2 * s + 1)
            out_ref[s] = jnp.where(low, a0, b1) + _roll(jnp.where(low, a1, b0))
            return carry

        lax.fori_loop(0, 63, pair, 0, unroll=3)
        a0, b0 = node(126)
        out_ref[63] = a0 + _roll(b0)


def down_kernel(core_ref, mine_ref, other_ref, field_ref, wide_ref, basis_ref, near_ref, near2_ref, out_ref, down):
    core = core_ref[0]
    low = _low(R)
    zero = jnp.zeros((R, 128), BF)
    first = jnp.where(core == 0, mine_ref[...], other_ref[...])
    second = jnp.where(core == 0, other_ref[...], mine_ref[...])
    upper = jnp.concatenate([first, _roll(first), second, _roll(second)], axis=0)
    upper = jnp.where(low, upper, 0.0).astype(BF)
    root = field_ref[63][:, :64] + _nt(upper, wide_ref[126 * 64 : 127 * 64, :])
    down[63] = jnp.concatenate([root, root], axis=1).astype(BF)
    for level in range(5, -1, -1):
        for q in range(SIZES[level + 1]):
            row = (FIRST[level] + 2 * q) * 64
            x = _pick_half(low, q % 2, down[SLOT[level + 1] + q // 2], zero)
            s = SLOT[level] + q
            down[s] = (field_ref[s] + _nt(x, wide_ref[row : row + 128, :])).astype(BF)
    for p in range(32):
        d = down[p]
        both = jnp.concatenate([d[:, :64], d[:, 64:]], axis=0)
        y = _nt(both, basis_ref[2 * p : 2 * p + 2].reshape(128, 64))
        lanes = slice(128 * p, 128 * p + 128)
        total = jnp.where(low, y[:R], y[R:]) + near_ref[:, lanes] + near2_ref[:, lanes].astype(F32)
        out_ref[:, lanes] = total.astype(BF)


def _call(body, outs, ins, scratch=(), grid=None, out_specs=None, name=None, flops=0, moved=0):
    single = not isinstance(outs, (list, tuple))
    shapes = [outs] if single else list(outs)
    extra = {}
    if grid is not None:
        extra["grid"] = grid
    vm = pl.BlockSpec(memory_space=pltpu.VMEM)
    specs = out_specs if out_specs is not None else [vm] * len(shapes)
    return pl.pallas_call(
        body,
        out_shape=shapes[0] if single else tuple(shapes),
        in_specs=ins,
        out_specs=specs[0] if single else tuple(specs),
        scratch_shapes=list(scratch),
        compiler_params=pltpu.CompilerParams(vmem_limit_bytes=VMEM_LIMIT),
        cost_estimate=pl.CostEstimate(flops=flops, bytes_accessed=moved, transcendentals=0),
        name=name,
        **extra,
    )


def shards(
    vectors,
    leaf_basis,
    local_transfer,
    coupling,
    coupling_source,
    top_transfer,
    top_coupling,
    top_target,
    top_source,
    near_blocks,
    near_source,
):
    n_leaf = lax.axis_size("leaf")
    me = lax.axis_index("leaf")
    core = (me % 2).astype(jnp.int32).reshape(1)
    vm = pl.BlockSpec(memory_space=pltpu.VMEM)
    sm = pl.BlockSpec(memory_space=pltpu.SMEM)
    S = jax.ShapeDtypeStruct
    pair = [(i, i ^ 1) for i in range(n_leaf)]
    up = [(i, i + 1) for i in range(n_leaf - 1)]
    back = [(i + 1, i) for i in range(n_leaf - 1)]
    swap = [(0, 1), (1, 0)]
    groups = [[2 * i + c for i in range(n_leaf // 2)] for c in range(2)]

    width = np.concatenate([np.full(n, n) for n in SIZES])
    first = np.concatenate([np.full(n, f) for n, f in zip(SIZES, FIRST)])
    shift = np.log2(width).astype(np.int32)
    width, first = jnp.asarray(width, jnp.int32)[None], jnp.asarray(first, jnp.int32)[None]
    shift = jnp.asarray(shift)[None]
    seen = coupling_source.T - (me - 1) * width
    field_ids = lax.shift_right_logical(seen, shift) * NODES + first + (seen & (width - 1))
    near_ids = near_source.T - (me - 1) * 64

    top_ids = jnp.concatenate([top_target, top_source])
    top_ids2 = lax.ppermute(top_ids, "leaf", pair)
    top_coupling2 = lax.ppermute(top_coupling, "leaf", pair)

    msg, root, wide = _call(
        up_kernel,
        (S((96, R, 128), BF), S((R, 128), F32), S((NODES * 64, 128), BF)),
        [vm, vm, vm],
        [pltpu.VMEM((NODES * 64, 128), F32)],
        name="up",
    )(vectors, leaf_basis, jnp.transpose(local_transfer, (1, 2, 0)))

    root2 = lax.ppermute(root, "leaf", pair)
    send = _call(pack_kernel, S((n_leaf // 2, 8, 128), BF), [sm, vm, vm], name="pack")(core, root, root2)
    before = lax.ppermute(msg, "leaf", up)
    after = lax.ppermute(msg, "leaf", back)
    gathered = lax.all_to_all(send, "leaf", 0, 0, tiled=True, axis_index_groups=groups)

    points = jnp.concatenate([before[64:], msg[64:], after[64:]], axis=0)
    points2 = lax.ppermute(points, "rhs", swap)

    partial = _call(
        upper_kernel,
        S((n_leaf // 2, 8, 128), BF),
        [sm, sm, vm, vm, vm, vm],
        [
            pltpu.VMEM((NODES * 64, 128), F32),
            pltpu.VMEM((64, 16, 128), BF),
            pltpu.VMEM((64, 16, 128), F32),
        ],
        name="upper",
    )(top_ids, top_ids2, gathered, jnp.transpose(top_transfer, (1, 2, 0)), top_coupling, top_coupling2)
    parts = lax.all_to_all(partial, "leaf", 0, 0, tiled=True, axis_index_groups=groups)
    mine = jnp.sum(parts.astype(F32), axis=0)
    other = lax.ppermute(mine, "leaf", pair)

    whole = lambda shape: pl.BlockSpec(shape, lambda i: (0,) * len(shape))
    near_mine, near_send = _call(
        near_kernel,
        (S((R, 4096), F32), S((R, 4096), BF)),
        [sm] + [whole((96, R, 128))] * 4 + [pl.BlockSpec((8, 4, 64, 64), lambda i: (i, 0, 0, 0))],
        [pltpu.VMEM((192, 64, 64), BF)],
        grid=(8,),
        out_specs=[pl.BlockSpec((R, 512), lambda i: (0, i))] * 2,
        name="near",
    )(near_ids, before, msg, after, points2, near_blocks)
    near_other = lax.ppermute(near_send, "rhs", swap)

    fields = _call(
        field_kernel,
        S((64, R, 128), F32),
        [sm]
        + [whole((96, R, 128))] * 3
        + [pl.BlockSpec((4, CHUNK, 64, 127), lambda i: (0, i, 0, 0))],
        [pltpu.VMEM((NODES * 128, 128), F32), pltpu.VMEM((3 * NODES, R, 128), BF)],
        grid=(64 // CHUNK,),
        out_specs=[whole((64, R, 128))],
        name="field",
    )(field_ids, before, msg, after, jnp.transpose(coupling, (1, 2, 3, 0)))

    return _call(
        down_kernel,
        S((R, 4096), BF),
        [sm] + [vm] * 7,
        [pltpu.VMEM((64, R, 128), BF)],
        name="down",
    )(core, mine, other, fields, wide, leaf_basis, near_mine, near_other)


def solution(mesh):
    placed = (
        P("rhs", "leaf"),
        P("leaf", None, None),
        P("leaf", None, None),
        P("leaf", None, None, None),
        P("leaf", None),
        P(),
        P("leaf", None, None),
        P("leaf"),
        P("leaf"),
        P("leaf", "rhs", None, None),
        P("leaf", "rhs"),
    )
    return jax.shard_map(
        shards, mesh=mesh, in_specs=placed, out_specs=P("rhs", "leaf"), check_vma=False
    )
```

time: 1460 us -> 114 us (0.08)
  waiting for transfers between devices: 1100 us -> 19 us
  local copies, waits for them, and re-layouts: 184 us -> 11.6 us
  matrix products: 49 us -> 0 us
  Pallas kernels: 0 us -> 45.3 us
  other arithmetic: 45 us -> 2.97 us
  between operations: 16.1 us -> 0.13 us
    psum x1 -> x0, waiting for transfers between devices: 1060 us -> none  [shards(): upper_field = lax.psum(partial_field, 'leaf')]
    unnamed x111 -> x38, local copies, waits for them, and re-layouts: 67.1 us -> 11.5 us
    dot_general x35 -> x0, matrix products: 49 us -> none  [the longest x5 11.3 us: descend(): jnp.einsum('rhb,hab->rha', parents, transfer_rows, precision=full_precision)]
    pallas_call x0 -> x6, Pallas kernels: none -> 45.3 us  [the longest x1 18 us: shards(): _call(field_kernel, S((64, R, 128), F32), [sm] + [whole((96, R, 128))] *...]
    slice x20 -> x3, local copies, waits for them, and re-layouts: 45 us -> 0.05 us  [shards(): points = jnp.concatenate([before[64:], msg[64:], after[64:]], axis=0)]
    all_gather x1 -> x0, waiting for transfers between devices: 39 us -> none  [shards(): root_terms = lax.all_gather(root_term, 'leaf', axis=1, tiled=True)]
    ppermute x16 -> x8, starting transfers between devices: 45.3 us -> 12 us  [the longest x1 5.14 us: shards(): after = lax.ppermute(msg, 'leaf', back)]
    gather x9 -> x0, local copies, waits for them, and re-layouts: 24.9 us -> none  [the longest x7 17.9 us: shards(): jnp.take(extended, source_ids.reshape(-1), axis=1)]
  transfers between devices with their start and end apart: 19 -> 10, of which waited for: 2 -> 5; matrix products, arithmetic and copies ran while one was open for 17% -> 2% of each run, Pallas kernels for 0% -> 31%
where the time goes in v1:
time: 114 us
  Pallas kernels  45.3 us (40%)
  starting transfers between devices  34.8 us (31%)
  waiting for transfers between devices  19 us (17%)
  local copies, waits for them, and re-layouts  11.6 us (10%)
  other arithmetic  2.97 us (3%)
    pallas_call x1, Pallas kernels, shards(): _call(field_kernel, S((64, R, 128), F32), [sm] + [whole((96, R, 128))] *...  18 us
    all_to_all x1, starting transfers between devices, shards(): lax.all_to_all(send, 'leaf', 0, 0, tiled=True, axis_index_groups=groups)  17.3 us
    unnamed x38, local copies, waits for them, and re-layouts  11.5 us
    pallas_call x1, Pallas kernels, shards(): _call(near_kernel, (S((R, 4096), F32), S((R, 4096), BF)), [sm] + [whole((...  8.64 us
    pallas_call x1, Pallas kernels, shards(): _call(upper_kernel, S((n_leaf // 2, 8, 128), BF), [sm, sm, vm, vm, vm, vm...  8.43 us
    all_to_all x1, waiting for transfers between devices, shards(): lax.all_to_all(send, 'leaf', 0, 0, tiled=True, axis_index_groups=groups)  7.8 us
    ppermute x1, waiting for transfers between devices, shards(): after = lax.ppermute(msg, 'leaf', back)  7.06 us
    pallas_call x1, Pallas kernels, shards(): _call(up_kernel, (S((96, R, 128), BF), S((R, 128), F32), S((NODES * 64, 1...  6.08 us
  transfers between devices with their start and end apart: 10, of which 5 were waited for; matrix products, arithmetic and copies ran while one was open for 2% of the time, Pallas kernels for 31%

profile of v1, /device:TPU:1, one launch (start us, length us, event | category | flops | bytes accessed | tf_op | source)
XLA Modules:
  0.0 113.8 jit_solution(17568089449780258465)
XLA Ops:
  0.0 1.2 %copy-done.2 = bf16[64,64,64]{2,1,0:T(8,128)(2,1)S(1)} copy-done((bf16[64,64,64]{2,1,0:T(8,128)(2,1)S(1)}, bf16[64,64,64]{2,1,0:T(8,128)(2,1)}, u32[]{:S(2)}) %copy-start.2) | copy-done | bytes 524312
  1.3 1.2 %copy-done.7 = bf16[127,64,64]{0,2,1:T(8,128)(2,1)S(1)} copy-done((bf16[127,64,64]{0,2,1:T(8,128)(2,1)S(1)}, bf16[127,64,64]{0,2,1:T(8,128)(2,1)}, u32[]{:S(2)}) %copy-start.7) | copy-done | bytes 1040408
  2.5 0.9 copy-done.11
  3.4 6.1 %up.1 = (bf16[96,32,128]{2,1,0:T(8,128)(2,1)S(1)}, f32[32,128]{1,0:T(8,128)S(1)}, bf16[8192,128]{1,0:T(8,128)(2,1)S(1)}) custom-call(bf16[32,4096]{1,0:T(8,128)(2,1)S(1)} %copy-done.11, bf16[64,64,64]{2,1,0:T(8,128)(2,1)S(1)} %copy-done.2, bf16[64,64,127]{2,1,0:T(8,128)(2,1)S(1)} %bitcast.10), custom_call_target="tpu_custom_call" | custom-call | tf_op jit(solution)/shard_map/up/pallas_call | solution.py:297
  9.5 1.4 %copy-done.4 = bf16[8192,128]{1,0:T(8,128)(2,1)} copy-done((bf16[8192,128]{1,0:T(8,128)(2,1)}, bf16[8192,128]{1,0:T(8,128)(2,1)S(1)}, u32[]{:S(2)}) %copy-start.4) | copy-done | bytes 2097176
  10.9 5.1 %collective-permute-start.5 = (bf16[96,32,128]{2,1,0:T(8,128)(2,1)S(1)}, bf16[96,32,128]{2,1,0:T(8,128)(2,1)S(1)}, u32[]{:S(2)}, u32[]{:S(2)}) collective-permute-start(bf16[96,32,128]{2,1,0:T(8,128)(2,1)S(1)} %get-tuple-element.11.own_ref), channel_id=1, source_target_pairs={{2,0},{4,2},{6,4},{8,6},{10,8},{12,10},{14,12},{16,14},{18,16},{20... | collective-permute-start | bytes 2359304 | tf_op jit(solution)/shard_map/ppermute | solution.py:308
  16.1 1.9 %collective-permute-start.4 = (bf16[96,32,128]{2,1,0:T(8,128)(2,1)S(1)}, bf16[96,32,128]{2,1,0:T(8,128)(2,1)S(1)}, u32[]{:S(2)}, u32[]{:S(2)}) collective-permute-start(bf16[96,32,128]{2,1,0:T(8,128)(2,1)S(1)} %get-tuple-element.11.own_ref), channel_id=1, source_target_pairs={{0,2},{2,4},{4,6},{6,8},{8,10},{10,12},{12,14},{14,16},{16,18},{18... | collective-permute-start | bytes 2359304 | tf_op jit(solution)/shard_map/ppermute | solution.py:307
  18.0 7.1 %collective-permute-done.5.right_ref = bf16[96,32,128]{2,1,0:T(8,128)(2,1)S(1)} collective-permute-done((bf16[96,32,128]{2,1,0:T(8,128)(2,1)S(1)}, bf16[96,32,128]{2,1,0:T(8,128)(2,1)S(1)}, u32[]{:S(2)}, u32[]{:S(2)}) %collective-permute-start.5) | collective-permute-done | bytes 786464 | tf_op jit(solution)/shard_map/ppermute | solution.py:308
  25.1 1.8 %collective-permute-done.4.left_ref = bf16[96,32,128]{2,1,0:T(8,128)(2,1)S(1)} collective-permute-done((bf16[96,32,128]{2,1,0:T(8,128)(2,1)S(1)}, bf16[96,32,128]{2,1,0:T(8,128)(2,1)S(1)}, u32[]{:S(2)}, u32[]{:S(2)}) %collective-permute-start.4) | collective-permute-done | bytes 786464 | tf_op jit(solution)/shard_map/ppermute | solution.py:307
  26.9 1.0 pad_maximum_fusion
  27.9 2.3 %collective-permute-start.6 = (bf16[96,32,128]{2,1,0:T(8,128)(2,1)}, bf16[96,32,128]{2,1,0:T(8,128)(2,1)}, u32[]{:S(2)}, u32[]{:S(2)}) collective-permute-start(bf16[96,32,128]{2,1,0:T(8,128)(2,1)} %pad_maximum_fusion), channel_id=1, source_target_pairs={{0,1},{1,0},{2,3},{3,2},{4,5},{5,4},{6,7},{7,6},{8,9},{9,8},{10,11... | collective-permute-start | bytes 2359304 | tf_op jit(solution)/shard_map/ppermute | solution.py:312
  30.2 1.2 %collective-permute-done.1.other_ref = f32[32,128]{1,0:T(8,128)S(1)} collective-permute-done((f32[32,128]{1,0:T(8,128)S(1)}, f32[32,128]{1,0:T(8,128)S(1)}, u32[]{:S(2)}, u32[]{:S(2)}) %collective-permute-start.1) | collective-permute-done | bytes 16416 | tf_op jit(solution)/shard_map/ppermute | solution.py:305
  31.4 0.6 copy-done.8
  32.0 17.3 %all-to-all-start = ((bf16[64,8,128]{2,1,0:T(8,128)(2,1)}), bf16[64,8,128]{2,1,0:T(8,128)(2,1)S(1)}, u32[]{:S(2)}, u32[]{:S(2)}) async-start(bf16[64,8,128]{2,1,0:T(8,128)(2,1)} %copy-done.8), calls=%async_computation | async-start | bytes 262144 | tf_op jit(solution)/shard_map/all_to_all | solution.py:309
  49.3 0.7 collective-permute-start.2
  50.0 0.1 pad_add_fusion.ids_ref
  50.2 1.1 collective-permute-done.ids2_ref
  51.3 7.8 %all-to-all-done.gathered_ref = bf16[64,8,128]{2,1,0:T(8,128)(2,1)S(1)} async-done(((bf16[64,8,128]{2,1,0:T(8,128)(2,1)}), bf16[64,8,128]{2,1,0:T(8,128)(2,1)S(1)}, u32[]{:S(2)}, u32[]{:S(2)}) %all-to-all-start) | async-done | bytes 131104 | tf_op jit(solution)/shard_map/all_to_all | solution.py:309
  59.1 0.8 copy-done.12
  59.9 8.4 %upper.1 = bf16[64,8,128]{2,1,0:T(8,128)(2,1)} custom-call(s32[8]{0:T(128)S(1)} %pad_add_fusion.ids_ref, s32[8]{0:T(128)S(1)} %collective-permute-done.ids2_ref, bf16[64,8,128]{2,1,0:T(8,128)(2,1)S(1)} %all-to-all-done.gathered_ref, bf16[64,64,126]{2,1,0:T(8,128)(2,1)S(1)} %bitcast.9, bf16[4,64,64]{2,1,0:T(8,128)(2,1)S(1)} %copy-done.12, ...), custom_call_target="tpu_custom_call" | custom-call | tf_op jit(solution)/shard_map/upper/pallas_call | solution.py:314
  68.4 5.5 %all-to-all-start.1 = ((bf16[64,8,128]{2,1,0:T(8,128)(2,1)}), bf16[64,8,128]{2,1,0:T(8,128)(2,1)S(1)}, u32[]{:S(2)}, u32[]{:S(2)}) async-start(bf16[64,8,128]{2,1,0:T(8,128)(2,1)} %upper.1), calls=%async_computation.1 | async-start | bytes 262144 | tf_op jit(solution)/shard_map/all_to_all | solution.py:325
  73.9 1.2 %broadcast_multiply_fusion = s32[127]{0:T(128)} fusion(s32[127]{0:T(128)} %constant.36.clone, s32[]{:T(128)S(6)} %sub.25), kind=kLoop, calls=%fused_computation.5 | loop fusion | flops 127 | bytes 1020 | tf_op jit(solution)/shard_map/mul | solution.py:289
  75.1 2.2 %copy-done = bf16[64,4,64,64]{3,2,1,0:T(8,128)(2,1)S(1)} copy-done((bf16[64,4,64,64]{3,2,1,0:T(8,128)(2,1)S(1)}, bf16[64,4,64,64]{3,2,1,0:T(8,128)(2,1)}, u32[]{:S(2)}) %copy-start) | copy-done | bytes 2097176
  77.3 8.6 %near.1 = (f32[32,4096]{1,0:T(8,128)S(1)}, bf16[32,4096]{1,0:T(8,128)(2,1)}) custom-call(s32[4,64]{1,0:T(4,128)S(1)} %subtract_bitcast_fusion.ids_ref, bf16[96,32,128]{2,1,0:T(8,128)(2,1)S(1)} %collective-permute-done.4.left_ref, bf16[96,32,128]{2,1,0:T(8,128)(2,1)S(1)} %get-tuple-element.11.own_ref, ...), custom_call_target="tpu_custom_call" | custom-call | tf_op jit(solution)/shard_map/near/pallas_call | solution.py:330
  85.9 0.8 copy-done.9
  86.7 1.0 collective-permute-start.7
  87.7 0.1 convert_reduce_fusion.mine_ref
  87.8 1.0 collective-permute-start.3
  88.8 0.7 add_bitcast_fusion.ids_ref
  89.4 2.2 %copy-done.1 = bf16[127,4,64,64]{0,3,2,1:T(8,128)(2,1)S(1)} copy-done((bf16[127,4,64,64]{0,3,2,1:T(8,128)(2,1)S(1)}, bf16[127,4,64,64]{0,3,2,1:T(8,128)(2,1)}, u32[]{:S(2)}) %copy-start.1) | copy-done | bytes 4161560
  91.6 18.0 %field.1.field_ref = f32[64,32,128]{2,1,0:T(8,128)S(1)} custom-call(s32[4,127]{1,0:T(4,128)S(1)} %add_bitcast_fusion.ids_ref, bf16[96,32,128]{2,1,0:T(8,128)(2,1)S(1)} %collective-permute-done.4.left_ref, bf16[96,32,128]{2,1,0:T(8,128)(2,1)S(1)} %get-tuple-element.11.own_ref, bf16[96,32,128]{2,1,0:T(8,128)(2,1)S(1)} %collective-permute-done.5.right_ref, ...), custom_call_target="tpu_custom_call" | custom-call | tf_op jit(solution)/shard_map/field/pallas_call | solution.py:341
  109.7 4.1 %down.1 = bf16[32,4096]{1,0:T(8,128)(2,1)} custom-call(s32[1]{0:T(128)} %bitcast.core_ref, f32[8,128]{1,0:T(8,128)S(1)} %convert_reduce_fusion.mine_ref, f32[8,128]{1,0:T(8,128)S(1)} %collective-permute-done.3.other_ref, f32[64,32,128]{2,1,0:T(8,128)S(1)} %field.1.field_ref, bf16[8192,128]{1,0:T(8,128)(2,1)S(1)} %copy-done.5, ...), custom_call_target="tpu_custom_call" | custom-call | tf_op jit(solution)/shard_map/down/pallas_call | solution.py:353
  (41 shorter events, 0.2 us)
Async XLA Ops:
  0.0 50.0 %copy-start.17 = (s32[4]{0:T(128)S(1)}, s32[4]{0:T(128)}, u32[]{:S(2)}) copy-start(s32[4]{0:T(128)} %param.22) | copy-start | bytes 52
  0.0 50.0 %copy-start.18 = (s32[4]{0:T(128)S(1)}, s32[4]{0:T(128)}, u32[]{:S(2)}) copy-start(s32[4]{0:T(128)} %param.21) | copy-start | bytes 52
  0.0 1.3 %copy-start.2 = (bf16[64,64,64]{2,1,0:T(8,128)(2,1)S(1)}, bf16[64,64,64]{2,1,0:T(8,128)(2,1)}, u32[]{:S(2)}) copy-start(bf16[64,64,64]{2,1,0:T(8,128)(2,1)} %basis_ref.3) | copy-start | bytes 1572868
  1.3 1.2 %copy-start.7 = (bf16[127,64,64]{0,2,1:T(8,128)(2,1)S(1)}, bf16[127,64,64]{0,2,1:T(8,128)(2,1)}, u32[]{:S(2)}) copy-start(bf16[127,64,64]{0,2,1:T(8,128)(2,1)} %param.16) | copy-start | bytes 3121156
  2.5 0.9 copy-start.11
  3.4 55.7 %copy-start.6 = (bf16[126,64,64]{0,2,1:T(8,128)(2,1)S(1)}, bf16[126,64,64]{0,2,1:T(8,128)(2,1)}, u32[]{:S(2)}) copy-start(bf16[126,64,64]{0,2,1:T(8,128)(2,1)} %param.19) | copy-start | bytes 3096580
  3.4 71.7 %copy-start.14 = (s32[64,4]{0,1:T(4,128)S(1)}, s32[64,4]{0,1:T(4,128)}, u32[]{:S(2)}) copy-start(s32[64,4]{0,1:T(4,128)} %param.24) | copy-start | bytes 3076
  9.5 1.4 %copy-start.4 = (bf16[8192,128]{1,0:T(8,128)(2,1)}, bf16[8192,128]{1,0:T(8,128)(2,1)S(1)}, u32[]{:S(2)}) copy-start(bf16[8192,128]{1,0:T(8,128)(2,1)S(1)} %get-tuple-element.12.wide_ref) | copy-start | bytes 6291460
  10.9 14.2 %collective-permute-start.5 = (bf16[96,32,128]{2,1,0:T(8,128)(2,1)S(1)}, bf16[96,32,128]{2,1,0:T(8,128)(2,1)S(1)}, u32[]{:S(2)}, u32[]{:S(2)}) collective-permute-start(bf16[96,32,128]{2,1,0:T(8,128)(2,1)S(1)} %get-tuple-element.11.own_ref), channel_id=1, source_target_pairs={{2,0},{4,2},{6,4},{8,6},{10,8},{12,10},{14,12},{16,14},{18,16},{20... | collective-permute-start | bytes 2359304 | tf_op jit(solution)/shard_map/ppermute | solution.py:308
  16.1 10.8 %collective-permute-start.4 = (bf16[96,32,128]{2,1,0:T(8,128)(2,1)S(1)}, bf16[96,32,128]{2,1,0:T(8,128)(2,1)S(1)}, u32[]{:S(2)}, u32[]{:S(2)}) collective-permute-start(bf16[96,32,128]{2,1,0:T(8,128)(2,1)S(1)} %get-tuple-element.11.own_ref), channel_id=1, source_target_pairs={{0,2},{2,4},{4,6},{6,8},{8,10},{10,12},{12,14},{14,16},{16,18},{18... | collective-permute-start | bytes 2359304 | tf_op jit(solution)/shard_map/ppermute | solution.py:307
  27.9 47.2 %collective-permute-start.6 = (bf16[96,32,128]{2,1,0:T(8,128)(2,1)}, bf16[96,32,128]{2,1,0:T(8,128)(2,1)}, u32[]{:S(2)}, u32[]{:S(2)}) collective-permute-start(bf16[96,32,128]{2,1,0:T(8,128)(2,1)} %pad_maximum_fusion), channel_id=1, source_target_pairs={{0,1},{1,0},{2,3},{3,2},{4,5},{5,4},{6,7},{7,6},{8,9},{9,8},{10,11... | collective-permute-start | bytes 2359304 | tf_op jit(solution)/shard_map/ppermute | solution.py:312
  30.2 1.2 %collective-permute-start.1 = (f32[32,128]{1,0:T(8,128)S(1)}, f32[32,128]{1,0:T(8,128)S(1)}, u32[]{:S(2)}, u32[]{:S(2)}) collective-permute-start(f32[32,128]{1,0:T(8,128)S(1)} %get-tuple-element.10.mine_ref), channel_id=1, source_target_pairs={{0,2},{2,0},{4,6},{6,4},{8,10},{10,8},{12,14},{14,12},{16,18},{18,... | collective-permute-start | bytes 49160 | tf_op jit(solution)/shard_map/ppermute | solution.py:305
  31.4 0.7 copy-start.8
  32.0 27.0 %all-to-all-start = ((bf16[64,8,128]{2,1,0:T(8,128)(2,1)}), bf16[64,8,128]{2,1,0:T(8,128)(2,1)S(1)}, u32[]{:S(2)}, u32[]{:S(2)}) async-start(bf16[64,8,128]{2,1,0:T(8,128)(2,1)} %copy-done.8), calls=%async_computation | async-start | bytes 262144 | tf_op jit(solution)/shard_map/all_to_all | solution.py:309
  49.3 2.0 %collective-permute-start.2 = (bf16[4,64,64]{2,1,0:T(8,128)(2,1)}, bf16[4,64,64]{2,1,0:T(8,128)(2,1)}, u32[]{:S(2)}, u32[]{:S(2)}) collective-permute-start(bf16[4,64,64]{2,1,0:T(8,128)(2,1)} %blocks_ref.2), channel_id=1, source_target_pairs={{0,2},{2,0},{4,6},{6,4},{8,10},{10,8},{12,14},{14,12},{16,18},{18,... | collective-permute-start | bytes 98312 | tf_op jit(solution)/shard_map/ppermute | solution.py:295
  50.1 1.1 %collective-permute-start = (s32[8]{0:T(128)S(1)}, s32[8]{0:T(128)S(1)}, u32[]{:S(2)}, u32[]{:S(2)}) collective-permute-start(s32[8]{0:T(128)S(1)} %pad_add_fusion.ids_ref), channel_id=1, source_target_pairs={{0,2},{2,0},{4,6},{6,4},{8,10},{10,8},{12,14},{14,12},{16,18},{18,... | collective-permute-start | bytes 104 | tf_op jit(solution)/shard_map/ppermute | solution.py:294
  59.1 0.8 copy-start.12
  68.4 20.4 %copy-start.13 = (s32[127,4]{0,1:T(4,128)S(1)}, s32[127,4]{0,1:T(4,128)}, u32[]{:S(2)}) copy-start(s32[127,4]{0,1:T(4,128)} %param.18) | copy-start | bytes 6100
  68.4 20.4 %copy-start.15 = (s32[127]{0:T(128)S(1)}, s32[127]{0:T(128)}, u32[]{:S(2)}) copy-start(s32[127]{0:T(128)} %constant.48) | copy-start | bytes 1528
  68.4 20.4 %copy-start.16 = (s32[127]{0:T(128)S(1)}, s32[127]{0:T(128)}, u32[]{:S(2)}) copy-start(s32[127]{0:T(128)} %constant.38.clone) | copy-start | bytes 1528
  68.4 19.3 %all-to-all-start.1 = ((bf16[64,8,128]{2,1,0:T(8,128)(2,1)}), bf16[64,8,128]{2,1,0:T(8,128)(2,1)S(1)}, u32[]{:S(2)}, u32[]{:S(2)}) async-start(bf16[64,8,128]{2,1,0:T(8,128)(2,1)} %upper.1), calls=%async_computation.1 | async-start | bytes 262144 | tf_op jit(solution)/shard_map/all_to_all | solution.py:325
  75.1 2.2 %copy-start = (bf16[64,4,64,64]{3,2,1,0:T(8,128)(2,1)S(1)}, bf16[64,4,64,64]{3,2,1,0:T(8,128)(2,1)}, u32[]{:S(2)}) copy-start(bf16[64,4,64,64]{3,2,1,0:T(8,128)(2,1)} %blocks_ref.3) | copy-start | bytes 6291460
  77.3 32.4 %copy-start.3 = (bf16[64,64,64]{2,1,0:T(8,128)(2,1)S(1)}, bf16[64,64,64]{2,1,0:T(8,128)(2,1)}, u32[]{:S(2)}) copy-start(bf16[64,64,64]{2,1,0:T(8,128)(2,1)} %basis_ref.3) | copy-start | bytes 1572868
  85.9 0.8 copy-start.9
  86.7 22.9 %collective-permute-start.7 = (bf16[32,4096]{1,0:T(8,128)(2,1)}, bf16[32,4096]{1,0:T(8,128)(2,1)}, u32[]{:S(2)}, u32[]{:S(2)}) collective-permute-start(bf16[32,4096]{1,0:T(8,128)(2,1)} %get-tuple-element.14), channel_id=1, source_target_pairs={{0,1},{1,0},{2,3},{3,2},{4,5},{5,4},{6,7},{7,6},{8,9},{9,8},{10,11... | collective-permute-start | bytes 786440 | tf_op jit(solution)/shard_map/ppermute | solution.py:339
  87.8 21.9 %collective-permute-start.3 = (f32[8,128]{1,0:T(8,128)S(1)}, f32[8,128]{1,0:T(8,128)S(1)}, u32[]{:S(2)}, u32[]{:S(2)}) collective-permute-start(f32[8,128]{1,0:T(8,128)S(1)} %convert_reduce_fusion.mine_ref), channel_id=1, source_target_pairs={{0,2},{2,0},{4,6},{6,4},{8,10},{10,8},{12,14},{14,12},{16,18},{18,... | collective-permute-start | bytes 12296 | tf_op jit(solution)/shard_map/ppermute | solution.py:327
  89.4 2.2 %copy-start.1 = (bf16[127,4,64,64]{0,3,2,1:T(8,128)(2,1)S(1)}, bf16[127,4,64,64]{0,3,2,1:T(8,128)(2,1)}, u32[]{:S(2)}) copy-start(bf16[127,4,64,64]{0,3,2,1:T(8,128)(2,1)} %param.17) | copy-start | bytes 12484612
  91.6 18.1 %copy-start.5 = (bf16[8192,128]{1,0:T(8,128)(2,1)S(1)}, bf16[8192,128]{1,0:T(8,128)(2,1)}, u32[]{:S(2)}) copy-start(bf16[8192,128]{1,0:T(8,128)(2,1)} %copy-done.4) | copy-start | bytes 6291460
  91.6 18.1 %copy-start.10 = (f32[32,4096]{1,0:T(8,128)S(1)}, f32[32,4096]{1,0:T(8,128)}, u32[]{:S(2)}) copy-start(f32[32,4096]{1,0:T(8,128)} %copy-done.9) | copy-start | bytes 1572868

commit v2 on v1

v2 whole, which is shorter than its diff:
```python
import jax
import jax.numpy as jnp
from jax import lax
from jax.experimental import pallas as pl
from jax.experimental.pallas import tpu as pltpu
from jax.sharding import PartitionSpec as P

BF = jnp.bfloat16
F32 = jnp.float32
MIB = 1024 * 1024

NODES = 128
SIZES = (64, 32, 16, 8, 4, 2, 1)
FIRST = (0, 64, 96, 112, 120, 124, 126)
SLOT = (0, 32, 48, 56, 60, 62, 63)
R = 32


def _nn(a, b):
    return lax.dot_general(a, b, (((1,), (0,)), ((), ())), preferred_element_type=F32)


def _nt(a, b):
    return lax.dot_general(a, b, (((1,), (1,)), ((), ())), preferred_element_type=F32)


def _low(rows):
    return lax.broadcasted_iota(jnp.int32, (rows, 128), 1) < 64


def _eye(lanes):
    row = lax.broadcasted_iota(jnp.int32, (128, lanes), 0)
    col = lax.broadcasted_iota(jnp.int32, (128, lanes), 1)
    return jnp.where(row == col, 1.0, 0.0).astype(BF)


def _pick_half(low, half, x, zero):
    return jnp.where(low == (half == 0), x, zero)


def _roll(x):
    return pltpu.roll(x, 64, 1)


PITCH = 72
PITCH_FIELD = 136


def _fetch(sems, *moves):
    copies = [pltpu.make_async_copy(src, dst, sems.at[i]) for i, (src, dst) in enumerate(moves)]
    for copy in copies:
        copy.start()
    return copies


def _chunks(src, dst, parts):
    size = src.shape[0] // parts
    return [
        (src.at[i * size : (i + 1) * size], dst.at[i * size : (i + 1) * size]) for i in range(parts)
    ]


def _unstack(raw_ref, wide, copies):
    eye = _eye(raw_ref.shape[2])
    size = 64 // len(copies)
    for k in range(64):
        if k % size == 0:
            copies[k // size].wait()
        block = raw_ref[k]
        both = jnp.concatenate([block, block], axis=0)
        wide[pl.ds(k, NODES, stride=PITCH), :] = _nt(eye, both)


def _narrow(wide, out_ref, nodes):
    for t in nodes:
        out_ref[64 * t : 64 * t + 64, :] = wide[PITCH * t : PITCH * t + 64, :].astype(BF)


def up_kernel(
    v_hbm, basis_hbm, raw_hbm, msg_ref, root_ref, wide_hbm, v_ref, basis_ref, raw_ref, wide, wide_ref, sems, out_sems
):
    copies = _fetch(sems, (v_hbm, v_ref), (basis_hbm, basis_ref), *_chunks(raw_hbm, raw_ref, 1))
    low = _low(R)
    zero = jnp.zeros((R, 128), BF)
    copies[0].wait()
    copies[1].wait()
    for p in range(32):
        v = v_ref[:, 128 * p : 128 * p + 128]
        msg_ref[64 + p] = v
        both = jnp.concatenate([jnp.where(low, v, zero), jnp.where(low, zero, v)], axis=0)
        y = _nn(both, basis_ref[2 * p : 2 * p + 2].reshape(128, 64))
        msg_ref[p] = jnp.concatenate([y[:R], y[R:]], axis=1).astype(BF)
    _unstack(raw_ref, wide, copies[2:])
    _narrow(wide, wide_ref, range(NODES))
    out = _fetch(out_sems, (wide_ref, wide_hbm))
    for level in range(1, 7):
        for s in range(max(1, SIZES[level] // 2)):
            parts = []
            for q in (2 * s, 2 * s + 1)[: min(2, SIZES[level])]:
                row = (FIRST[level - 1] + 2 * q) * 64
                parts.append(_nn(msg_ref[SLOT[level - 1] + q], wide_ref[row : row + 128, :]))
            value = parts[0] if len(parts) == 1 else jnp.where(low, parts[0], parts[1])
            msg_ref[SLOT[level] + s] = value.astype(BF)
    root_ref[...] = _nn(msg_ref[63][:, :64], wide_ref[126 * 64 : 127 * 64, :])
    out[0].wait()


def pack_kernel(me_ref, mine_ref, other_ref, blocks_ref, target_ref, source_ref, out_ref):
    core = me_ref[0] % 2
    total = mine_ref[...] + other_ref[...]
    half = jnp.where(core == 0, total[:16], total[16:])
    packed = jnp.where(_low(8), half[:8], half[8:]).astype(BF)
    out_ref[...] = jnp.broadcast_to(packed[None], out_ref.shape)


def sum_kernel(parts_ref, out_ref):
    out_ref[...] = jnp.sum(parts_ref[...].astype(F32), axis=0)


def bundle_kernel(msg_ref, other_ref, done_ref, gathered_ref, out_ref):
    for s in range(32):
        out_ref[s] = other_ref[:, 128 * s : 128 * s + 128]


def top_kernel(raw_hbm, send_hbm, wide_hbm, done_ref, raw_ref, wide, wide_ref, sems, out_sems):
    copies = _fetch(sems, (raw_hbm, raw_ref))
    _unstack(raw_ref, wide, copies)
    _narrow(wide, wide_ref, range(NODES))
    out = _fetch(out_sems, (wide_ref, wide_hbm))
    done_ref[...] = jnp.zeros((8, 128), F32)
    out[0].wait()


def upper_kernel(
    target_ref, source_ref, target2_ref, source2_ref, gathered_ref, wide_hbm, blocks_hbm, blocks2_hbm, out_ref, wide, blocks_ref, coef, field, sems
):
    copies = _fetch(
        sems,
        (wide_hbm, wide),
        (blocks_hbm, blocks_ref.at[0:4]),
        (blocks2_hbm, blocks_ref.at[4:8]),
    )
    low8, low = _low(8), _low(16)
    zero = jnp.zeros((16, 128), BF)
    zero32 = jnp.zeros((16, 128), F32)
    for s in range(32):
        a, b = gathered_ref[2 * s].astype(F32), gathered_ref[2 * s + 1].astype(F32)
        top = jnp.where(low8, a, _roll(b))
        bottom = jnp.where(low8, _roll(a), b)
        coef[32 + s] = jnp.concatenate([top, bottom], axis=0).astype(BF)
    field[...] = jnp.zeros_like(field)
    copies[0].wait()
    size = 32
    while size >= 2:
        for s in range(size // 2, size):
            parts = []
            for h in (2 * s, 2 * s + 1):
                row = (2 * h - 2) * 64
                parts.append(_nn(coef[h], wide[row : row + 128, :]))
            coef[s] = jnp.where(low, parts[0], parts[1]).astype(BF)
        size //= 2
    copies[1].wait()
    copies[2].wait()
    for b in range(8):
        target = target_ref[b] if b < 4 else target2_ref[b - 4]
        source = source_ref[b] if b < 4 else source2_ref[b - 4]
        block = blocks_ref[b]
        block = jnp.concatenate([block, block], axis=0)
        block = jnp.concatenate([block, block], axis=1)
        x = _pick_half(low, source % 2, coef[source // 2], zero)
        field[target // 2] += _pick_half(low, target % 2, _nn(x, block), zero32)
    for h in range(2, 64):
        row = (2 * h - 2) * 64
        x = _pick_half(low, h % 2, field[h // 2].astype(BF), zero)
        field[h] += _nt(x, wide[row : row + 128, :])
    for s in range(32):
        x = field[32 + s]
        top, bottom = x[:8], x[8:]
        out_ref[2 * s] = jnp.where(low8, top, _roll(bottom)).astype(BF)
        out_ref[2 * s + 1] = jnp.where(low8, _roll(top), bottom).astype(BF)


def near_kernel(
    me_ref, ids_ref, inner_hbm, own_hbm, own2_hbm, outer_hbm, blocks_hbm, mine_out, other_out, halo, own, blocks_ref, leaves, sems
):
    copies = _fetch(
        sems,
        (own_hbm, own.at[0:R]),
        (own2_hbm, own.at[R:]),
        (inner_hbm.at[64:128], halo.at[0]),
        (outer_hbm.at[64:128], halo.at[1]),
        *_chunks(blocks_hbm, blocks_ref, 2),
    )
    for copy in copies[:4]:
        copy.wait()
    core = me_ref[0] % 2
    for s in range(32):
        for part in range(3):
            if part == 1:
                z = own[:, 128 * s : 128 * s + 128]
            else:
                side = 1 - core if part == 0 else core
                z = jnp.concatenate([halo[side, s], halo[side, 32 + s]], axis=0)
            e = 64 * part + 2 * s
            leaves[e] = z[:, :64]
            leaves[e + 1] = z[:, 64:]
    start = (me_ref[0] - 1) * 64
    for p in range(32):
        if p % (32 // 2) == 0:
            copies[4 + p // (32 // 2)].wait()
        parts = []
        for i in (2 * p, 2 * p + 1):
            total = _nt(leaves[ids_ref[0, i] - start], blocks_ref[i, 0])
            for j in range(1, 4):
                total += _nt(leaves[ids_ref[j, i] - start], blocks_ref[i, j])
            parts.append(total)
        pair = jnp.concatenate(parts, axis=1)
        mine_out[:, 128 * p : 128 * p + 128] = pair[:R]
        other_out[:, 128 * p : 128 * p + 128] = pair[R:].astype(BF)


def field_kernel(me_ref, ids_ref, inner_hbm, own_hbm, outer_hbm, raw_hbm, out_ref, raw_ref, wide, seen, coef, sems):
    copies = _fetch(
        sems,
        (inner_hbm.at[0:64], seen.at[0]),
        (own_hbm.at[0:64], seen.at[1]),
        (outer_hbm.at[0:64], seen.at[2]),
        *[(raw_hbm.at[:, 32 * i : 32 * i + 32], raw_ref.at[:, 32 * i : 32 * i + 32]) for i in range(2)],
    )
    low = _low(R)
    core = me_ref[0] % 2
    for copy in copies[:3]:
        copy.wait()
    for part in range(3):
        side = (2 - 2 * core, 1, 2 * core)[part]
        for s in range(64):
            x = seen[side, s]
            y = jnp.concatenate([x[:, 64:], x[:, :64]], axis=1)
            coef[part * NODES + 2 * s] = jnp.where(low, x, y)
            coef[part * NODES + 2 * s + 1] = jnp.where(low, y, x)
    eye = _eye(raw_ref.shape[3])
    for m in range(64):
        if m % 32 == 0:
            copies[3 + m // 32].wait()
        for k in range(2):
            both = jnp.concatenate([raw_ref[k, m], raw_ref[k + 2, m]], axis=0)
            wide[pl.ds(k * 64 + m, NODES, stride=PITCH_FIELD), :] = _nt(eye, both)
    before = me_ref[0] - 1

    def source(k, t):
        level = next(i for i in range(7) if t < FIRST[i] + SIZES[i])
        e = ids_ref[k, t] - before * SIZES[level]
        part = lax.shift_right_logical(e, 6 - level)
        return coef[part * NODES + (e & (SIZES[level] - 1)) + FIRST[level]]

    def node(t):
        a = jnp.where(low, source(0, t), source(1, t))
        b = jnp.where(low, source(2, t), source(3, t))
        y = _nn(jnp.concatenate([a, b], axis=0), wide[PITCH_FIELD * t : PITCH_FIELD * t + 128, :].astype(BF))
        return y[:R], y[R:]

    for s in range(63):
        a0, b0 = node(2 * s)
        a1, b1 = node(2 * s + 1)
        out_ref[s] = jnp.where(low, a0, b1) + _roll(jnp.where(low, a1, b0))
    a0, b0 = node(126)
    out_ref[63] = a0 + _roll(b0)


def down_kernel(
    me_ref, mine_ref, other_ref, field_ref, wide_hbm, basis_hbm, near_ref, near2_ref, out_ref, down, wide_ref, basis_ref, sems
):
    rows = (NODES * 64, 96 * 64, 64 * 64, 32 * 64, 0)
    spans = [(b, a) for a, b in zip(rows, rows[1:])]
    copies = _fetch(
        sems,
        *[(wide_hbm.at[a:b], wide_ref.at[a:b]) for a, b in spans],
        *_chunks(basis_hbm, basis_ref, 2),
    )
    core = me_ref[0] % 2
    low = _low(R)
    zero = jnp.zeros((R, 128), BF)
    first = jnp.where(core == 0, mine_ref[...], other_ref[...])
    second = jnp.where(core == 0, other_ref[...], mine_ref[...])
    upper = jnp.concatenate([first, _roll(first), second, _roll(second)], axis=0)
    upper = jnp.where(low, upper, 0.0).astype(BF)
    copies[0].wait()
    root = field_ref[63][:, :64] + _nt(upper, wide_ref[126 * 64 : 127 * 64, :])
    down[63] = jnp.concatenate([root, root], axis=1).astype(BF)
    for level in range(5, -1, -1):
        for q in range(SIZES[level + 1]):
            if level == 1 and q == 0:
                copies[1].wait()
            if level == 0 and q % 16 == 0:
                copies[3 - q // 16].wait()
            row = (FIRST[level] + 2 * q) * 64
            x = _pick_half(low, q % 2, down[SLOT[level + 1] + q // 2], zero)
            s = SLOT[level] + q
            down[s] = (field_ref[s] + _nt(x, wide_ref[row : row + 128, :])).astype(BF)
    for p in range(32):
        if p % 16 == 0:
            copies[4 + p // 16].wait()
        d = down[p]
        both = jnp.concatenate([d[:, :64], d[:, 64:]], axis=0)
        y = _nt(both, basis_ref[2 * p : 2 * p + 2].reshape(128, 64))
        lanes = slice(128 * p, 128 * p + 128)
        total = jnp.where(low, y[:R], y[R:]) + near_ref[:, lanes] + near2_ref[:, lanes].astype(F32)
        out_ref[:, lanes] = total.astype(BF)


def _call(body, name, outs, ins, scratch, limit, micros, out_specs=None):
    vm = pl.BlockSpec(memory_space=pltpu.VMEM)
    if out_specs is None:
        out_specs = (vm,) * len(outs) if isinstance(outs, tuple) else vm
    return pl.pallas_call(
        body,
        out_shape=outs,
        in_specs=ins,
        out_specs=out_specs,
        scratch_shapes=scratch,
        compiler_params=pltpu.CompilerParams(vmem_limit_bytes=limit * MIB),
        cost_estimate=pl.CostEstimate(
            flops=int(micros * 1.0e9), bytes_accessed=int(micros * 3.0e6), transcendentals=0
        ),
        name=name,
    )


def shards(
    vectors,
    leaf_basis,
    local_transfer,
    coupling,
    coupling_source,
    top_transfer,
    top_coupling,
    top_target,
    top_source,
    near_blocks,
    near_source,
):
    n_leaf = lax.axis_size("leaf")
    me = lax.axis_index("leaf").astype(jnp.int32).reshape(1)
    vm = pl.BlockSpec(memory_space=pltpu.VMEM)
    sm = pl.BlockSpec(memory_space=pltpu.SMEM)
    S = jax.ShapeDtypeStruct
    pair = [(i, i ^ 1) for i in range(n_leaf)]
    across = [(i, i + 1) for i in range(1, n_leaf - 1, 2)]
    across += [(j, i) for i, j in across]
    swap = [(0, 1), (1, 0)]
    groups = [[2 * i + c for i in range(n_leaf // 2)] for c in range(2)]

    vectors2 = lax.ppermute(vectors, "rhs", swap)
    top_target2 = lax.ppermute(top_target, "leaf", pair)
    top_source2 = lax.ppermute(top_source, "leaf", pair)
    top_coupling2 = lax.ppermute(top_coupling, "leaf", pair)

    hbm = pl.BlockSpec(memory_space=pltpu.HBM)
    any_ = pl.BlockSpec(memory_space=pl.ANY)
    dma = pltpu.SemaphoreType.DMA
    V = pltpu.VMEM
    raw = jnp.transpose(local_transfer, (1, 2, 0))
    msg, root, wide = _call(
        up_kernel,
        "up",
        (S((128, R, 128), BF), S((R, 128), F32), S((NODES * 64, 128), BF)),
        [hbm, hbm, hbm],
        [
            V(vectors.shape, BF),
            V(leaf_basis.shape, BF),
            V(raw.shape, BF),
            V((NODES * PITCH, 128), F32),
            V((NODES * 64, 128), BF),
            dma((6,)),
            dma((1,)),
        ],
        60,
        4,
        (vm, vm, hbm),
    )(vectors, leaf_basis, raw)

    root2 = lax.ppermute(root, "leaf", pair)
    send = _call(pack_kernel, "pack", S((n_leaf // 2, 8, 128), BF), [sm, vm, vm, any_, any_, any_], [], 4, 0.5)(
        me, root, root2, top_coupling2, top_target2, top_source2
    )
    gathered = lax.all_to_all(send, "leaf", 0, 0, tiled=True, axis_index_groups=groups)

    raw = jnp.transpose(top_transfer, (1, 2, 0))
    wide_top, done = _call(
        top_kernel,
        "top",
        (S((NODES * 64, 128), BF), S((8, 128), F32)),
        [hbm, any_],
        [
            V(raw.shape, BF),
            V((NODES * PITCH, 128), F32),
            V((NODES * 64, 128), BF),
            dma((1,)),
            dma((1,)),
        ],
        57,
        4,
        (hbm, vm),
    )(raw, send)

    msg = pl.pallas_call(
        bundle_kernel,
        grid=(1,),
        out_shape=S((128, R, 128), BF),
        in_specs=[any_, vm, any_, any_],
        out_specs=pl.BlockSpec((32, R, 128), lambda i: (3, 0, 0)),
        input_output_aliases={0: 0},
        compiler_params=pltpu.CompilerParams(vmem_limit_bytes=4 * MIB),
        cost_estimate=pl.CostEstimate(flops=0, bytes_accessed=1000000, transcendentals=0),
        name="bundle",
    )(msg, vectors2, done, gathered)
    inner = lax.ppermute(msg, "leaf", pair)
    outer = lax.ppermute(msg, "leaf", across)
    partial = _call(
        upper_kernel,
        "upper",
        S((n_leaf // 2, 8, 128), BF),
        [sm, sm, sm, sm, vm, hbm, any_, any_],
        [
            V((NODES * 64, 128), BF),
            V((8, 64, 64), BF),
            V((64, 16, 128), BF),
            V((64, 16, 128), F32),
            dma((3,)),
        ],
        57,
        6,
    )(top_target, top_source, top_target2, top_source2, gathered, wide_top, top_coupling, top_coupling2)
    parts = lax.all_to_all(partial, "leaf", 0, 0, tiled=True, axis_index_groups=groups)

    near_mine, near_send = _call(
        near_kernel,
        "near",
        (S((R, 4096), F32), S((R, 4096), BF)),
        [sm, sm, any_, any_, any_, any_, hbm],
        [
            V((2, 64, R, 128), BF),
            V((2 * R, 4096), BF),
            V(near_blocks.shape, BF),
            V((192, 64, 64), BF),
            dma((12,)),
        ],
        52,
        5,
    )(me, near_source.T, inner, vectors, vectors2, outer, near_blocks)
    near_other = lax.ppermute(near_send, "rhs", swap)
    parts, near_mine = lax.optimization_barrier((parts, near_mine))
    mine = _call(sum_kernel, "total", S((8, 128), F32), [vm], [], 4, 0.5)(parts)
    other = lax.ppermute(mine, "leaf", pair)

    raw = jnp.transpose(coupling, (1, 2, 3, 0))
    fields = _call(
        field_kernel,
        "field",
        S((64, R, 128), F32),
        [sm, sm, any_, any_, any_, hbm],
        [
            V(raw.shape, BF),
            V((NODES * PITCH_FIELD, 128), F32),
            V((3, 64, R, 128), BF),
            V((3 * NODES, R, 128), BF),
            dma((5,)),
        ],
        52,
        8,
    )(me, coupling_source.T, inner, msg, outer, raw)

    return _call(
        down_kernel,
        "down",
        S((R, 4096), BF),
        [sm, vm, vm, vm, hbm, hbm, vm, vm],
        [V((64, R, 128), BF), V((NODES * 64, 128), BF), V(leaf_basis.shape, BF), dma((6,))],
        10,
        4,
    )(me, mine, other, fields, wide, leaf_basis, near_mine, near_other)


def solution(mesh):
    placed = (
        P("rhs", "leaf"),
        P("leaf", None, None),
        P("leaf", None, None),
        P("leaf", None, None, None),
        P("leaf", None),
        P(),
        P("leaf", None, None),
        P("leaf"),
        P("leaf"),
        P("leaf", "rhs", None, None),
        P("leaf", "rhs"),
    )
    return jax.shard_map(
        shards, mesh=mesh, in_specs=placed, out_specs=P("rhs", "leaf"), check_vma=False
    )
```

time: 114 us -> 79.8 us (0.70)
  waiting for transfers between devices: 19 us -> 8.85 us
  Pallas kernels: 45.3 us -> 35.2 us
  local copies, waits for them, and re-layouts: 11.6 us -> 2.44 us
  other arithmetic: 2.97 us -> 0 us
  starting transfers between devices: 34.8 us -> 32.4 us
    pallas_call x6 -> x9, Pallas kernels: 45.3 us -> 35.2 us  [the longest x1 8.25 us: shards(): _call(field_kernel, 'field', S((64, R, 128), F32), [sm, sm, any_, any_, a...]
    unnamed x38 -> x32, local copies, waits for them, and re-layouts: 11.5 us -> 2.44 us
    ppermute x4 -> x5, waiting for transfers between devices: 9.95 us -> 1.03 us  [the longest x1 0.72 us: shards(): top_target2 = lax.ppermute(top_target, 'leaf', pair)]
    all_to_all x1, starting transfers between devices: 17.3 us -> 11.8 us  [shards(): lax.all_to_all(send, 'leaf', 0, 0, tiled=True, axis_index_groups=groups)]
    ppermute x4 -> x5, starting transfers between devices: 9.39 us -> 6.16 us  [the longest x1 4.03 us: shards(): outer = lax.ppermute(msg, 'leaf', across)]
    all_to_all x1, waiting for transfers between devices: 7.8 us -> 4.62 us  [shards(): lax.all_to_all(send, 'leaf', 0, 0, tiled=True, axis_index_groups=groups)]
    all_to_all x1, waiting for transfers between devices: 0.01 us -> 3.18 us  [shards(): lax.all_to_all(partial, 'leaf', 0, 0, tiled=True, axis_index_groups=groups)]
    ppermute x1, starting transfers between devices: 0.71 us -> 3.24 us  [shards(): top_coupling2 = lax.ppermute(top_coupling, 'leaf', pair)]
  transfers between devices with their start and end apart: 10 -> 11, of which waited for: 5 -> 4; matrix products, arithmetic and copies ran while one was open for 2% -> 0% of each run, Pallas kernels for 31% -> 39%
where the time goes in v2:
time: 79.8 us; the launch traced here: 79.4 us
  Pallas kernels  35.2 us (44%)
  starting transfers between devices  32.4 us (41%)
  waiting for transfers between devices  8.85 us (11%)
  local copies, waits for them, and re-layouts  2.44 us (3%)
    all_to_all x1, starting transfers between devices, shards(): lax.all_to_all(send, 'leaf', 0, 0, tiled=True, axis_index_groups=groups)  11.8 us
    pallas_call x1, Pallas kernels, shards(): _call(field_kernel, 'field', S((64, R, 128), F32), [sm, sm, any_, any_, a...  8.25 us
    all_to_all x1, starting transfers between devices, shards(): lax.all_to_all(partial, 'leaf', 0, 0, tiled=True, axis_index_groups=groups)  7.44 us
    pallas_call x1, Pallas kernels, shards(): _call(up_kernel, 'up', (S((128, R, 128), BF), S((R, 128), F32), S((NODES...  6.11 us
    pallas_call x1, Pallas kernels, shards(): _call(upper_kernel, 'upper', S((n_leaf // 2, 8, 128), BF), [sm, sm, sm, s...  5.68 us
    pallas_call x1, Pallas kernels, shards(): _call(near_kernel, 'near', (S((R, 4096), F32), S((R, 4096), BF)), [sm, sm...  5.37 us
    pallas_call x1, Pallas kernels, shards(): _call(top_kernel, 'top', (S((NODES * 64, 128), BF), S((8, 128), F32)), [h...  5.08 us
    all_to_all x1, waiting for transfers between devices, shards(): lax.all_to_all(send, 'leaf', 0, 0, tiled=True, axis_index_groups=groups)  4.62 us
  transfers between devices with their start and end apart: 11, of which 4 were waited for; matrix products, arithmetic and copies ran while one was open for 0% of the time, Pallas kernels for 39%

profile of v2, /device:TPU:1, one launch (start us, length us, event | category | flops | bytes accessed | tf_op | source)
XLA Modules:
  0.0 79.4 jit_solution(16643425494709491027)
XLA Ops:
  0.0 3.2 %collective-permute-start.3 = (bf16[4,64,64]{2,1,0:T(8,128)(2,1)}, bf16[4,64,64]{2,1,0:T(8,128)(2,1)S(1)}, u32[]{:S(2)}, u32[]{:S(2)}) collective-permute-start(bf16[4,64,64]{2,1,0:T(8,128)(2,1)} %blocks_hbm.2), channel_id=1, source_target_pairs={{0,2},{2,0},{4,6},{6,4},{8,10},{10,8},{12,14},{14,12},{16,18},{18,... | collective-permute-start | bytes 98312 | tf_op jit(solution)/shard_map/ppermute | solution.py:356
  3.2 6.1 %up.1 = (bf16[128,32,128]{2,1,0:T(8,128)(2,1)}, f32[32,128]{1,0:T(8,128)}, bf16[8192,128]{1,0:T(8,128)(2,1)}) custom-call(bf16[32,4096]{1,0:T(8,128)(2,1)} %own_hbm.1, bf16[64,64,64]{2,1,0:T(8,128)(2,1)} %basis_hbm.3, bf16[64,64,127]{2,1,0:T(8,128)(2,1)} %bitcast.9), custom_call_target="tpu_custom_call" | custom-call | flops 4000000000 | bytes 12000000 | tf_op jit(solution)/shard_map/up/pallas_call | solution.py:363
  9.4 0.1 collective-permute-start.2
  9.5 1.3 %collective-permute-start.4 = (bf16[32,4096]{1,0:T(8,128)(2,1)S(1)}, bf16[32,4096]{1,0:T(8,128)(2,1)S(1)}, u32[]{:S(2)}, u32[]{:S(2)}) collective-permute-start(bf16[32,4096]{1,0:T(8,128)(2,1)S(1)} %copy-done.5), channel_id=1, source_target_pairs={{0,1},{1,0},{2,3},{3,2},{4,5},{5,4},{6,7},{7,6},{8,9},{9,8},{10,11... | collective-permute-start | bytes 786440 | tf_op jit(solution)/shard_map/ppermute | solution.py:353
  10.7 0.7 collective-permute-start
  11.4 0.1 collective-permute-start.1
  11.5 0.7 collective-permute-done.target_ref.target2_ref
  12.2 0.3 collective-permute-done.1.source_ref.source2_ref
  12.6 0.0 collective-permute-done.3.blocks_ref.blocks2_hbm
  12.6 0.0 copy-start.7
  12.6 0.7 copy-done.7
  13.3 0.7 pack.1.send_hbm
  14.0 11.8 %all-to-all-start = ((bf16[64,8,128]{2,1,0:T(8,128)(2,1)}), bf16[64,8,128]{2,1,0:T(8,128)(2,1)S(1)}, u32[]{:S(2)}, u32[]{:S(2)}) async-start(bf16[64,8,128]{2,1,0:T(8,128)(2,1)} %pack.1.send_hbm), calls=%async_computation | async-start | bytes 262144 | tf_op jit(solution)/shard_map/all_to_all | solution.py:386
  25.8 5.1 %top.1 = (bf16[8192,128]{1,0:T(8,128)(2,1)}, f32[8,128]{1,0:T(8,128)}) custom-call(bf16[64,64,126]{2,1,0:T(8,128)(2,1)} %bitcast.10, bf16[64,8,128]{2,1,0:T(8,128)(2,1)} %pack.1.send_hbm), custom_call_target="tpu_custom_call" | custom-call | flops 4000000000 | bytes 12000000 | tf_op jit(solution)/shard_map/top/pallas_call | solution.py:389
  30.9 0.0 collective-permute-done.4.other_ref.own2_hbm
  30.9 4.6 %all-to-all-done.gathered_ref = bf16[64,8,128]{2,1,0:T(8,128)(2,1)S(1)} async-done(((bf16[64,8,128]{2,1,0:T(8,128)(2,1)}), bf16[64,8,128]{2,1,0:T(8,128)(2,1)S(1)}, u32[]{:S(2)}, u32[]{:S(2)}) %all-to-all-start) | async-done | bytes 131104 | tf_op jit(solution)/shard_map/all_to_all | solution.py:386
  35.5 0.7 copy-done.3
  36.3 4.0 %collective-permute-start.6 = (bf16[128,32,128]{2,1,0:T(8,128)(2,1)S(1)}, bf16[128,32,128]{2,1,0:T(8,128)(2,1)S(1)}, u32[]{:S(2)}, u32[]{:S(2)}) collective-permute-start(bf16[128,32,128]{2,1,0:T(8,128)(2,1)S(1)} %bundle.1.own_hbm), channel_id=1, source_target_pairs={{2,4},{6,8},{10,12},{14,16},{18,20},{22,24},{26,28},{30,32},{34,36... | collective-permute-start | bytes 3145736 | tf_op jit(solution)/shard_map/ppermute | solution.py:418
  40.3 0.1 collective-permute-start.5
  40.4 0.0 copy-start.8
  40.4 5.7 %upper.1 = bf16[64,8,128]{2,1,0:T(8,128)(2,1)} custom-call(s32[4]{0:T(128)} %target_ref.1, s32[4]{0:T(128)} %source_ref.1, s32[4]{0:T(128)} %copy-done.10, s32[4]{0:T(128)} %copy-done.11, bf16[64,8,128]{2,1,0:T(8,128)(2,1)} %copy-done.2, bf16[8192,128]{1,0:T(8,128)(2,1)} %get-tuple-element.15.wide_hbm, bf16[4,64,64]{2,1,0:T(8,128)(2,1)} %blocks_hbm.2, ...), custom_call_target="tpu_custom_call" | custom-call | flops 6000000000 | bytes 18000000 | tf_op jit(solution)/shard_map/upper/pallas_call | solution.py:419
  46.1 7.4 %all-to-all-start.1 = ((bf16[64,8,128]{2,1,0:T(8,128)(2,1)}), bf16[64,8,128]{2,1,0:T(8,128)(2,1)S(1)}, u32[]{:S(2)}, u32[]{:S(2)}) async-start(bf16[64,8,128]{2,1,0:T(8,128)(2,1)} %upper.1), calls=%async_computation.1 | async-start | bytes 262144 | tf_op jit(solution)/shard_map/all_to_all | solution.py:434
  53.6 0.0 collective-permute-done.6.outer_hbm
  53.6 0.0 collective-permute-done.5.inner_hbm
  53.6 1.0 %copy-done.13 = bf16[128,32,128]{2,1,0:T(8,128)(2,1)} copy-done((bf16[128,32,128]{2,1,0:T(8,128)(2,1)}, bf16[128,32,128]{2,1,0:T(8,128)(2,1)S(1)}, u32[]{:S(2)}) %copy-start.13) | copy-done | bytes 1048600
  54.6 5.4 %near.1 = (f32[32,4096]{1,0:T(8,128)S(1)}, bf16[32,4096]{1,0:T(8,128)(2,1)S(1)}) custom-call(s32[1]{0:T(128)} %bitcast.me_ref, s32[4,64]{1,0:T(4,128)S(1)} %bitcast.6, bf16[128,32,128]{2,1,0:T(8,128)(2,1)} %collective-permute-done.5.inner_hbm, bf16[32,4096]{1,0:T(8,128)(2,1)S(1)} %copy-done.5, ...), custom_call_target="tpu_custom_call" | custom-call | flops 5000000000 | bytes 15000000 | tf_op jit(solution)/shard_map/near/pallas_call | solution.py:436
  60.0 3.2 %all-to-all-done.1.parts_ref = bf16[64,8,128]{2,1,0:T(8,128)(2,1)S(1)} async-done(((bf16[64,8,128]{2,1,0:T(8,128)(2,1)}), bf16[64,8,128]{2,1,0:T(8,128)(2,1)S(1)}, u32[]{:S(2)}, u32[]{:S(2)}) %all-to-all-start.1) | async-done | bytes 131104 | tf_op jit(solution)/shard_map/all_to_all | solution.py:434
  63.2 0.1 total.1.mine_ref
  63.2 2.1 %collective-permute-start.7 = (f32[8,128]{1,0:T(8,128)S(1)}, f32[8,128]{1,0:T(8,128)S(1)}, u32[]{:S(2)}, u32[]{:S(2)}) collective-permute-start(f32[8,128]{1,0:T(8,128)S(1)} %total.1.mine_ref), channel_id=1, source_target_pairs={{0,2},{2,0},{4,6},{6,4},{8,10},{10,8},{12,14},{14,12},{16,18},{18,... | collective-permute-start | bytes 12296 | tf_op jit(solution)/shard_map/ppermute | solution.py:454
  65.4 1.6 %collective-permute-start.8 = (bf16[32,4096]{1,0:T(8,128)(2,1)S(1)}, bf16[32,4096]{1,0:T(8,128)(2,1)S(1)}, u32[]{:S(2)}, u32[]{:S(2)}) collective-permute-start(bf16[32,4096]{1,0:T(8,128)(2,1)S(1)} %get-tuple-element.22), channel_id=1, source_target_pairs={{0,1},{1,0},{2,3},{3,2},{4,5},{5,4},{6,7},{7,6},{8,9},{9,8},{10,11... | collective-permute-start | bytes 786440 | tf_op jit(solution)/shard_map/ppermute | solution.py:451
  67.0 8.3 %field.1.field_ref = f32[64,32,128]{2,1,0:T(8,128)S(1)} custom-call(s32[1]{0:T(128)} %bitcast.me_ref, s32[4,127]{1,0:T(4,128)S(1)} %bitcast.7, bf16[128,32,128]{2,1,0:T(8,128)(2,1)} %collective-permute-done.5.inner_hbm, bf16[128,32,128]{2,1,0:T(8,128)(2,1)} %copy-done.1, bf16[128,32,128]{2,1,0:T(8,128)(2,1)} %copy-done.13, bf16[4,64,64,127]{3,2,1,0:T(8,128)(2,1)} %bitcast.8), custom_call_target="tpu_custom_call" | custom-call | flops 8000000000 | bytes 24000000 | tf_op jit(solution)/shard_map/field/pallas_call | solution.py:457
  75.3 4.0 %down.1 = bf16[32,4096]{1,0:T(8,128)(2,1)} custom-call(s32[1]{0:T(128)} %bitcast.me_ref, f32[8,128]{1,0:T(8,128)S(1)} %total.1.mine_ref, f32[8,128]{1,0:T(8,128)S(1)} %collective-permute-done.7.other_ref, f32[64,32,128]{2,1,0:T(8,128)S(1)} %field.1.field_ref, bf16[8192,128]{1,0:T(8,128)(2,1)S(1)} %copy-done.12, bf16[64,64,64]{2,1,0:T(8,128)(2,1)S(1)} %copy-done.4, ...), custom_call_target="tpu_custom_call" | custom-call | flops 4000000000 | bytes 12000000 | tf_op jit(solution)/shard_map/down/pallas_call | solution.py:473
  (31 shorter events, 0.1 us)
Async XLA Ops:
  0.0 12.6 %collective-permute-start.3 = (bf16[4,64,64]{2,1,0:T(8,128)(2,1)}, bf16[4,64,64]{2,1,0:T(8,128)(2,1)S(1)}, u32[]{:S(2)}, u32[]{:S(2)}) collective-permute-start(bf16[4,64,64]{2,1,0:T(8,128)(2,1)} %blocks_hbm.2), channel_id=1, source_target_pairs={{0,2},{2,0},{4,6},{6,4},{8,10},{10,8},{12,14},{14,12},{16,18},{18,... | collective-permute-start | bytes 98312 | tf_op jit(solution)/shard_map/ppermute | solution.py:356
  3.2 6.2 %copy-start.5 = (bf16[32,4096]{1,0:T(8,128)(2,1)S(1)}, bf16[32,4096]{1,0:T(8,128)(2,1)}, u32[]{:S(2)}) copy-start(bf16[32,4096]{1,0:T(8,128)(2,1)} %own_hbm.1) | copy-start | bytes 786436
  3.2 7.5 %copy-start.14 = (s32[4]{0:T(128)S(1)}, s32[4]{0:T(128)}, u32[]{:S(2)}) copy-start(s32[4]{0:T(128)} %target_ref.1) | copy-start | bytes 52
  3.2 8.2 %copy-start.15 = (s32[4]{0:T(128)S(1)}, s32[4]{0:T(128)}, u32[]{:S(2)}) copy-start(s32[4]{0:T(128)} %source_ref.1) | copy-start | bytes 52
  9.4 3.2 %collective-permute-start.2 = (f32[32,128]{1,0:T(8,128)}, f32[32,128]{1,0:T(8,128)S(1)}, u32[]{:S(2)}, u32[]{:S(2)}) collective-permute-start(f32[32,128]{1,0:T(8,128)} %get-tuple-element.14.mine_ref), channel_id=1, source_target_pairs={{0,2},{2,0},{4,6},{6,4},{8,10},{10,8},{12,14},{14,12},{16,18},{18,... | collective-permute-start | bytes 49160 | tf_op jit(solution)/shard_map/ppermute | solution.py:382
  9.5 21.4 %collective-permute-start.4 = (bf16[32,4096]{1,0:T(8,128)(2,1)S(1)}, bf16[32,4096]{1,0:T(8,128)(2,1)S(1)}, u32[]{:S(2)}, u32[]{:S(2)}) collective-permute-start(bf16[32,4096]{1,0:T(8,128)(2,1)S(1)} %copy-done.5), channel_id=1, source_target_pairs={{0,1},{1,0},{2,3},{3,2},{4,5},{5,4},{6,7},{7,6},{8,9},{9,8},{10,11... | collective-permute-start | bytes 786440 | tf_op jit(solution)/shard_map/ppermute | solution.py:353
  10.7 1.5 %collective-permute-start = (s32[4]{0:T(128)S(1)}, s32[4]{0:T(128)S(1)}, u32[]{:S(2)}, u32[]{:S(2)}) collective-permute-start(s32[4]{0:T(128)S(1)} %copy-done.14), channel_id=1, source_target_pairs={{0,2},{2,0},{4,6},{6,4},{8,10},{10,8},{12,14},{14,12},{16,18},{18,... | collective-permute-start | bytes 56 | tf_op jit(solution)/shard_map/ppermute | solution.py:354
  11.4 1.1 %collective-permute-start.1 = (s32[4]{0:T(128)S(1)}, s32[4]{0:T(128)S(1)}, u32[]{:S(2)}, u32[]{:S(2)}) collective-permute-start(s32[4]{0:T(128)S(1)} %copy-done.15), channel_id=1, source_target_pairs={{0,2},{2,0},{4,6},{6,4},{8,10},{10,8},{12,14},{14,12},{16,18},{18,... | collective-permute-start | bytes 56 | tf_op jit(solution)/shard_map/ppermute | solution.py:355
  12.2 18.6 %copy-start.10 = (s32[4]{0:T(128)}, s32[4]{0:T(128)S(1)}, u32[]{:S(2)}) copy-start(s32[4]{0:T(128)S(1)} %collective-permute-done.target_ref.target2_ref) | copy-start | bytes 52
  12.6 18.3 %copy-start.11 = (s32[4]{0:T(128)}, s32[4]{0:T(128)S(1)}, u32[]{:S(2)}) copy-start(s32[4]{0:T(128)S(1)} %collective-permute-done.1.source_ref.source2_ref) | copy-start | bytes 52
  12.6 18.3 %copy-start.6 = (bf16[4,64,64]{2,1,0:T(8,128)(2,1)}, bf16[4,64,64]{2,1,0:T(8,128)(2,1)S(1)}, u32[]{:S(2)}) copy-start(bf16[4,64,64]{2,1,0:T(8,128)(2,1)S(1)} %collective-permute-done.3.blocks_ref.blocks2_hbm) | copy-start | bytes 98308
  12.6 0.7 copy-start.7
  14.0 21.5 %all-to-all-start = ((bf16[64,8,128]{2,1,0:T(8,128)(2,1)}), bf16[64,8,128]{2,1,0:T(8,128)(2,1)S(1)}, u32[]{:S(2)}, u32[]{:S(2)}) async-start(bf16[64,8,128]{2,1,0:T(8,128)(2,1)} %pack.1.send_hbm), calls=%async_computation | async-start | bytes 262144 | tf_op jit(solution)/shard_map/all_to_all | solution.py:386
  25.8 9.8 %copy-start = (bf16[128,32,128]{2,1,0:T(8,128)(2,1)S(1)}, bf16[128,32,128]{2,1,0:T(8,128)(2,1)}, u32[]{:S(2)}) copy-start(bf16[128,32,128]{2,1,0:T(8,128)(2,1)} %get-tuple-element.16.msg_ref) | copy-start | bytes 3145732
  35.5 4.9 %copy-start.2 = (bf16[64,8,128]{2,1,0:T(8,128)(2,1)}, bf16[64,8,128]{2,1,0:T(8,128)(2,1)S(1)}, u32[]{:S(2)}) copy-start(bf16[64,8,128]{2,1,0:T(8,128)(2,1)S(1)} %all-to-all-done.gathered_ref) | copy-start | bytes 393220
  35.5 0.7 copy-start.3
  36.3 9.9 %copy-start.1 = (bf16[128,32,128]{2,1,0:T(8,128)(2,1)}, bf16[128,32,128]{2,1,0:T(8,128)(2,1)S(1)}, u32[]{:S(2)}) copy-start(bf16[128,32,128]{2,1,0:T(8,128)(2,1)S(1)} %bundle.1.own_hbm) | copy-start | bytes 3145732
  36.3 17.3 %collective-permute-start.6 = (bf16[128,32,128]{2,1,0:T(8,128)(2,1)S(1)}, bf16[128,32,128]{2,1,0:T(8,128)(2,1)S(1)}, u32[]{:S(2)}, u32[]{:S(2)}) collective-permute-start(bf16[128,32,128]{2,1,0:T(8,128)(2,1)S(1)} %bundle.1.own_hbm), channel_id=1, source_target_pairs={{2,4},{6,8},{10,12},{14,16},{18,20},{22,24},{26,28},{30,32},{34,36... | collective-permute-start | bytes 3145736 | tf_op jit(solution)/shard_map/ppermute | solution.py:418
  40.3 13.3 %collective-permute-start.5 = (bf16[128,32,128]{2,1,0:T(8,128)(2,1)S(1)}, bf16[128,32,128]{2,1,0:T(8,128)(2,1)}, u32[]{:S(2)}, u32[]{:S(2)}) collective-permute-start(bf16[128,32,128]{2,1,0:T(8,128)(2,1)S(1)} %bundle.1.own_hbm), channel_id=1, source_target_pairs={{0,2},{2,0},{4,6},{6,4},{8,10},{10,8},{12,14},{14,12},{16,18},{18,... | collective-permute-start | bytes 3145736 | tf_op jit(solution)/shard_map/ppermute | solution.py:417
  40.4 14.2 %copy-start.8 = (s32[64,4]{0,1:T(4,128)S(1)}, s32[64,4]{0,1:T(4,128)}, u32[]{:S(2)}) copy-start(s32[64,4]{0,1:T(4,128)} %param.21) | copy-start | bytes 3076
  46.1 17.0 %all-to-all-start.1 = ((bf16[64,8,128]{2,1,0:T(8,128)(2,1)}), bf16[64,8,128]{2,1,0:T(8,128)(2,1)S(1)}, u32[]{:S(2)}, u32[]{:S(2)}) async-start(bf16[64,8,128]{2,1,0:T(8,128)(2,1)} %upper.1), calls=%async_computation.1 | async-start | bytes 262144 | tf_op jit(solution)/shard_map/all_to_all | solution.py:434
  53.6 1.0 %copy-start.13 = (bf16[128,32,128]{2,1,0:T(8,128)(2,1)}, bf16[128,32,128]{2,1,0:T(8,128)(2,1)S(1)}, u32[]{:S(2)}) copy-start(bf16[128,32,128]{2,1,0:T(8,128)(2,1)S(1)} %collective-permute-done.6.outer_hbm) | copy-start | bytes 3145732
  54.6 12.4 %copy-start.9 = (s32[127,4]{0,1:T(4,128)S(1)}, s32[127,4]{0,1:T(4,128)}, u32[]{:S(2)}) copy-start(s32[127,4]{0,1:T(4,128)} %param.15) | copy-start | bytes 6100
  63.2 12.0 %collective-permute-start.7 = (f32[8,128]{1,0:T(8,128)S(1)}, f32[8,128]{1,0:T(8,128)S(1)}, u32[]{:S(2)}, u32[]{:S(2)}) collective-permute-start(f32[8,128]{1,0:T(8,128)S(1)} %total.1.mine_ref), channel_id=1, source_target_pairs={{0,2},{2,0},{4,6},{6,4},{8,10},{10,8},{12,14},{14,12},{16,18},{18,... | collective-permute-start | bytes 12296 | tf_op jit(solution)/shard_map/ppermute | solution.py:454
  65.4 9.9 %collective-permute-start.8 = (bf16[32,4096]{1,0:T(8,128)(2,1)S(1)}, bf16[32,4096]{1,0:T(8,128)(2,1)S(1)}, u32[]{:S(2)}, u32[]{:S(2)}) collective-permute-start(bf16[32,4096]{1,0:T(8,128)(2,1)S(1)} %get-tuple-element.22), channel_id=1, source_target_pairs={{0,1},{1,0},{2,3},{3,2},{4,5},{5,4},{6,7},{7,6},{8,9},{9,8},{10,11... | collective-permute-start | bytes 786440 | tf_op jit(solution)/shard_map/ppermute | solution.py:451
  67.0 8.3 %copy-start.4 = (bf16[64,64,64]{2,1,0:T(8,128)(2,1)S(1)}, bf16[64,64,64]{2,1,0:T(8,128)(2,1)}, u32[]{:S(2)}) copy-start(bf16[64,64,64]{2,1,0:T(8,128)(2,1)} %basis_hbm.3) | copy-start | bytes 1572868
  67.0 8.3 %copy-start.12 = (bf16[8192,128]{1,0:T(8,128)(2,1)S(1)}, bf16[8192,128]{1,0:T(8,128)(2,1)}, u32[]{:S(2)}) copy-start(bf16[8192,128]{1,0:T(8,128)(2,1)} %get-tuple-element.20.wide_hbm) | copy-start | bytes 6291460

commit v3 on v2

--- a/solution.py
+++ b/solution.py
@@ -28,12 +28,6 @@
     return lax.broadcasted_iota(jnp.int32, (rows, 128), 1) < 64
 
 
-def _eye(lanes):
-    row = lax.broadcasted_iota(jnp.int32, (128, lanes), 0)
-    col = lax.broadcasted_iota(jnp.int32, (128, lanes), 1)
-    return jnp.where(row == col, 1.0, 0.0).astype(BF)
-
-
 def _pick_half(low, half, x, zero):
     return jnp.where(low == (half == 0), x, zero)
 
@@ -60,39 +54,39 @@
     ]
 
 
-def _unstack(raw_ref, wide, copies):
-    eye = _eye(raw_ref.shape[2])
-    size = 64 // len(copies)
+def _unstack(raw_ref, wide, copy):
+    copy.wait()
     for k in range(64):
-        if k % size == 0:
-            copies[k // size].wait()
-        block = raw_ref[k]
+        block = raw_ref[k].astype(F32)
         both = jnp.concatenate([block, block], axis=0)
-        wide[pl.ds(k, NODES, stride=PITCH), :] = _nt(eye, both)
+        wide[pl.ds(k, raw_ref.shape[2], stride=PITCH), :] = both.T
 
 
 def _narrow(wide, out_ref, nodes):
-    for t in nodes:
+    for t in range(nodes):
         out_ref[64 * t : 64 * t + 64, :] = wide[PITCH * t : PITCH * t + 64, :].astype(BF)
 
 
 def up_kernel(
-    v_hbm, basis_hbm, raw_hbm, msg_ref, root_ref, wide_hbm, v_ref, basis_ref, raw_ref, wide, wide_ref, sems, out_sems
+    v_hbm, basis_hbm, raw_hbm, msg_hbm, root_ref, wide_hbm, v_ref, basis_ref, raw_ref, msg_ref, wide, wide_ref, sems, out_sems
 ):
-    copies = _fetch(sems, (v_hbm, v_ref), (basis_hbm, basis_ref), *_chunks(raw_hbm, raw_ref, 1))
+    copies = _fetch(sems, (raw_hbm, raw_ref), (v_hbm, v_ref), (basis_hbm, basis_ref))
     low = _low(R)
     zero = jnp.zeros((R, 128), BF)
-    copies[0].wait()
+    _unstack(raw_ref, wide, copies[0])
+    _narrow(wide, wide_ref, raw_ref.shape[2])
+    out = _fetch(out_sems, (wide_ref, wide_hbm))
     copies[1].wait()
+    copies[2].wait()
     for p in range(32):
         v = v_ref[:, 128 * p : 128 * p + 128]
         msg_ref[64 + p] = v
         both = jnp.concatenate([jnp.where(low, v, zero), jnp.where(low, zero, v)], axis=0)
         y = _nn(both, basis_ref[2 * p : 2 * p + 2].reshape(128, 64))
         msg_ref[p] = jnp.concatenate([y[:R], y[R:]], axis=1).astype(BF)
-    _unstack(raw_ref, wide, copies[2:])
-    _narrow(wide, wide_ref, range(NODES))
-    out = _fetch(out_sems, (wide_ref, wide_hbm))
+    out += _fetch(
+        out_sems.at[1:3], (msg_ref.at[0:32], msg_hbm.at[0:32]), (msg_ref.at[64:96], msg_hbm.at[64:96])
+    )
     for level in range(1, 7):
         for s in range(max(1, SIZES[level] // 2)):
             parts = []
@@ -101,12 +95,14 @@
                 parts.append(_nn(msg_ref[SLOT[level - 1] + q], wide_ref[row : row + 128, :]))
             value = parts[0] if len(parts) == 1 else jnp.where(low, parts[0], parts[1])
             msg_ref[SLOT[level] + s] = value.astype(BF)
+    out += _fetch(out_sems.at[3:4], (msg_ref.at[32:64], msg_hbm.at[32:64]))
     root_ref[...] = _nn(msg_ref[63][:, :64], wide_ref[126 * 64 : 127 * 64, :])
-    out[0].wait()
-
-
-def pack_kernel(me_ref, mine_ref, other_ref, blocks_ref, target_ref, source_ref, out_ref):
-    core = me_ref[0] % 2
+    for copy in out:
+        copy.wait()
+
+
+def pack_kernel(me_ref, mine_ref, other_ref, out_ref):
+    core = me_ref[0] & 1
     total = mine_ref[...] + other_ref[...]
     half = jnp.where(core == 0, total[:16], total[16:])
     packed = jnp.where(_low(8), half[:8], half[8:]).astype(BF)
@@ -117,17 +113,16 @@
     out_ref[...] = jnp.sum(parts_ref[...].astype(F32), axis=0)
 
 
-def bundle_kernel(msg_ref, other_ref, done_ref, gathered_ref, out_ref):
+def bundle_kernel(msg_ref, other_ref, gathered_ref, out_ref):
     for s in range(32):
         out_ref[s] = other_ref[:, 128 * s : 128 * s + 128]
 
 
-def top_kernel(raw_hbm, send_hbm, wide_hbm, done_ref, raw_ref, wide, wide_ref, sems, out_sems):
+def top_kernel(raw_hbm, msg_hbm, send_hbm, block_hbm, target_hbm, source_hbm, wide_hbm, msg_out, raw_ref, wide, wide_ref, sems, out_sems):
     copies = _fetch(sems, (raw_hbm, raw_ref))
-    _unstack(raw_ref, wide, copies)
-    _narrow(wide, wide_ref, range(NODES))
+    _unstack(raw_ref, wide, copies[0])
+    _narrow(wide, wide_ref, raw_ref.shape[2])
     out = _fetch(out_sems, (wide_ref, wide_hbm))
-    done_ref[...] = jnp.zeros((8, 128), F32)
     out[0].wait()
 
 
@@ -136,7 +131,8 @@
 ):
     copies = _fetch(
         sems,
-        (wide_hbm, wide),
+        (wide_hbm.at[62 * 64 :], wide.at[62 * 64 :]),
+        (wide_hbm.at[: 62 * 64], wide.at[: 62 * 64]),
         (blocks_hbm, blocks_ref.at[0:4]),
         (blocks2_hbm, blocks_ref.at[4:8]),
     )
@@ -144,7 +140,7 @@
     zero = jnp.zeros((16, 128), BF)
     zero32 = jnp.zeros((16, 128), F32)
     for s in range(32):
-        a, b = gathered_ref[2 * s].astype(F32), gathered_ref[2 * s + 1].astype(F32)
+        a, b = gathered_ref[63 - 2 * s].astype(F32), gathered_ref[62 - 2 * s].astype(F32)
         top = jnp.where(low8, a, _roll(b))
         bottom = jnp.where(low8, _roll(a), b)
         coef[32 + s] = jnp.concatenate([top, bottom], axis=0).astype(BF)
@@ -152,6 +148,8 @@
     copies[0].wait()
     size = 32
     while size >= 2:
+        if size == 16:
+            copies[1].wait()
         for s in range(size // 2, size):
             parts = []
             for h in (2 * s, 2 * s + 1):
@@ -159,16 +157,16 @@
                 parts.append(_nn(coef[h], wide[row : row + 128, :]))
             coef[s] = jnp.where(low, parts[0], parts[1]).astype(BF)
         size //= 2
-    copies[1].wait()
     copies[2].wait()
+    copies[3].wait()
     for b in range(8):
         target = target_ref[b] if b < 4 else target2_ref[b - 4]
         source = source_ref[b] if b < 4 else source2_ref[b - 4]
         block = blocks_ref[b]
         block = jnp.concatenate([block, block], axis=0)
         block = jnp.concatenate([block, block], axis=1)
-        x = _pick_half(low, source % 2, coef[source // 2], zero)
-        field[target // 2] += _pick_half(low, target % 2, _nn(x, block), zero32)
+        x = _pick_half(low, source & 1, coef[source >> 1], zero)
+        field[target >> 1] += _pick_half(low, target & 1, _nn(x, block), zero32)
     for h in range(2, 64):
         row = (2 * h - 2) * 64
         x = _pick_half(low, h % 2, field[h // 2].astype(BF), zero)
@@ -176,8 +174,8 @@
     for s in range(32):
         x = field[32 + s]
         top, bottom = x[:8], x[8:]
-        out_ref[2 * s] = jnp.where(low8, top, _roll(bottom)).astype(BF)
-        out_ref[2 * s + 1] = jnp.where(low8, _roll(top), bottom).astype(BF)
+        out_ref[63 - 2 * s] = jnp.where(low8, top, _roll(bottom)).astype(BF)
+        out_ref[62 - 2 * s] = jnp.where(low8, _roll(top), bottom).astype(BF)
 
 
 def near_kernel(
@@ -193,7 +191,7 @@
     )
     for copy in copies[:4]:
         copy.wait()
-    core = me_ref[0] % 2
+    core = me_ref[0] & 1
     for s in range(32):
         for part in range(3):
             if part == 1:
@@ -228,7 +226,7 @@
         *[(raw_hbm.at[:, 32 * i : 32 * i + 32], raw_ref.at[:, 32 * i : 32 * i + 32]) for i in range(2)],
     )
     low = _low(R)
-    core = me_ref[0] % 2
+    core = me_ref[0] & 1
     for copy in copies[:3]:
         copy.wait()
     for part in range(3):
@@ -238,13 +236,12 @@
             y = jnp.concatenate([x[:, 64:], x[:, :64]], axis=1)
             coef[part * NODES + 2 * s] = jnp.where(low, x, y)
             coef[part * NODES + 2 * s + 1] = jnp.where(low, y, x)
-    eye = _eye(raw_ref.shape[3])
     for m in range(64):
         if m % 32 == 0:
             copies[3 + m // 32].wait()
         for k in range(2):
-            both = jnp.concatenate([raw_ref[k, m], raw_ref[k + 2, m]], axis=0)
-            wide[pl.ds(k * 64 + m, NODES, stride=PITCH_FIELD), :] = _nt(eye, both)
+            both = jnp.concatenate([raw_ref[k, m], raw_ref[k + 2, m]], axis=0).astype(F32)
+            wide[pl.ds(k * 64 + m, raw_ref.shape[3], stride=PITCH_FIELD), :] = both.T
     before = me_ref[0] - 1
 
     def source(k, t):
@@ -267,39 +264,23 @@
     out_ref[63] = a0 + _roll(b0)
 
 
-def down_kernel(
-    me_ref, mine_ref, other_ref, field_ref, wide_hbm, basis_hbm, near_ref, near2_ref, out_ref, down, wide_ref, basis_ref, sems
-):
-    rows = (NODES * 64, 96 * 64, 64 * 64, 32 * 64, 0)
-    spans = [(b, a) for a, b in zip(rows, rows[1:])]
-    copies = _fetch(
-        sems,
-        *[(wide_hbm.at[a:b], wide_ref.at[a:b]) for a, b in spans],
-        *_chunks(basis_hbm, basis_ref, 2),
-    )
-    core = me_ref[0] % 2
+def down_kernel(me_ref, mine_ref, other_ref, field_ref, wide_ref, basis_ref, near_ref, near2_ref, out_ref, down):
+    core = me_ref[0] & 1
     low = _low(R)
     zero = jnp.zeros((R, 128), BF)
     first = jnp.where(core == 0, mine_ref[...], other_ref[...])
     second = jnp.where(core == 0, other_ref[...], mine_ref[...])
     upper = jnp.concatenate([first, _roll(first), second, _roll(second)], axis=0)
     upper = jnp.where(low, upper, 0.0).astype(BF)
-    copies[0].wait()
     root = field_ref[63][:, :64] + _nt(upper, wide_ref[126 * 64 : 127 * 64, :])
     down[63] = jnp.concatenate([root, root], axis=1).astype(BF)
     for level in range(5, -1, -1):
         for q in range(SIZES[level + 1]):
-            if level == 1 and q == 0:
-                copies[1].wait()
-            if level == 0 and q % 16 == 0:
-                copies[3 - q // 16].wait()
             row = (FIRST[level] + 2 * q) * 64
             x = _pick_half(low, q % 2, down[SLOT[level + 1] + q // 2], zero)
             s = SLOT[level] + q
             down[s] = (field_ref[s] + _nt(x, wide_ref[row : row + 128, :])).astype(BF)
     for p in range(32):
-        if p % 16 == 0:
-            copies[4 + p // 16].wait()
         d = down[p]
         both = jnp.concatenate([d[:, :64], d[:, 64:]], axis=0)
         y = _nt(both, basis_ref[2 * p : 2 * p + 2].reshape(128, 64))
@@ -308,7 +289,7 @@
         out_ref[:, lanes] = total.astype(BF)
 
 
-def _call(body, name, outs, ins, scratch, limit, micros, out_specs=None):
+def _call(body, name, outs, ins, scratch, limit, micros, out_specs=None, aliases={}):
     vm = pl.BlockSpec(memory_space=pltpu.VMEM)
     if out_specs is None:
         out_specs = (vm,) * len(outs) if isinstance(outs, tuple) else vm
@@ -318,6 +299,7 @@
         in_specs=ins,
         out_specs=out_specs,
         scratch_shapes=scratch,
+        input_output_aliases=aliases,
         compiler_params=pltpu.CompilerParams(vmem_limit_bytes=limit * MIB),
         cost_estimate=pl.CostEstimate(
             flops=int(micros * 1.0e9), bytes_accessed=int(micros * 3.0e6), transcendentals=0
@@ -348,12 +330,7 @@
     across = [(i, i + 1) for i in range(1, n_leaf - 1, 2)]
     across += [(j, i) for i, j in across]
     swap = [(0, 1), (1, 0)]
-    groups = [[2 * i + c for i in range(n_leaf // 2)] for c in range(2)]
-
-    vectors2 = lax.ppermute(vectors, "rhs", swap)
-    top_target2 = lax.ppermute(top_target, "leaf", pair)
-    top_source2 = lax.ppermute(top_source, "leaf", pair)
-    top_coupling2 = lax.ppermute(top_coupling, "leaf", pair)
+    groups = [[2 * i + c for i in reversed(range(n_leaf // 2))] for c in range(2)]
 
     hbm = pl.BlockSpec(memory_space=pltpu.HBM)
     any_ = pl.BlockSpec(memory_space=pl.ANY)
@@ -369,28 +346,36 @@
             V(vectors.shape, BF),
             V(leaf_basis.shape, BF),
             V(raw.shape, BF),
+            V((96, R, 128), BF),
             V((NODES * PITCH, 128), F32),
             V((NODES * 64, 128), BF),
-            dma((6,)),
-            dma((1,)),
+            dma((3,)),
+            dma((4,)),
         ],
-        60,
+        59,
         4,
-        (vm, vm, hbm),
+        (hbm, vm, hbm),
     )(vectors, leaf_basis, raw)
 
     root2 = lax.ppermute(root, "leaf", pair)
-    send = _call(pack_kernel, "pack", S((n_leaf // 2, 8, 128), BF), [sm, vm, vm, any_, any_, any_], [], 4, 0.5)(
-        me, root, root2, top_coupling2, top_target2, top_source2
+    send = _call(pack_kernel, "pack", S((n_leaf // 2, 8, 128), BF), [sm, vm, vm], [], 4, 0.5)(
+        me, root, root2
     )
     gathered = lax.all_to_all(send, "leaf", 0, 0, tiled=True, axis_index_groups=groups)
+    vectors2 = lax.ppermute(vectors, "rhs", swap)
+    block, target, source, _ = lax.optimization_barrier(
+        (top_coupling, top_target, top_source, send)
+    )
+    top_coupling2 = lax.ppermute(block, "leaf", pair)
+    top_target2 = lax.ppermute(target, "leaf", pair)
+    top_source2 = lax.ppermute(source, "leaf", pair)
 
     raw = jnp.transpose(top_transfer, (1, 2, 0))
-    wide_top, done = _call(
+    wide_top, msg = _call(
         top_kernel,
         "top",
-        (S((NODES * 64, 128), BF), S((8, 128), F32)),
-        [hbm, any_],
+        (S((NODES * 64, 128), BF), S((128, R, 128), BF)),
+        [hbm] + [any_] * 5,
         [
             V(raw.shape, BF),
             V((NODES * PITCH, 128), F32),
@@ -400,20 +385,21 @@
         ],
         57,
         4,
-        (hbm, vm),
-    )(raw, send)
+        (hbm, any_),
+        {1: 1},
+    )(raw, msg, send, top_coupling2, top_target2, top_source2)
 
     msg = pl.pallas_call(
         bundle_kernel,
         grid=(1,),
         out_shape=S((128, R, 128), BF),
-        in_specs=[any_, vm, any_, any_],
+        in_specs=[any_, vm, any_],
         out_specs=pl.BlockSpec((32, R, 128), lambda i: (3, 0, 0)),
         input_output_aliases={0: 0},
         compiler_params=pltpu.CompilerParams(vmem_limit_bytes=4 * MIB),
         cost_estimate=pl.CostEstimate(flops=0, bytes_accessed=1000000, transcendentals=0),
         name="bundle",
-    )(msg, vectors2, done, gathered)
+    )(msg, vectors2, gathered)
     inner = lax.ppermute(msg, "leaf", pair)
     outer = lax.ppermute(msg, "leaf", across)
     partial = _call(
@@ -426,7 +412,7 @@
             V((8, 64, 64), BF),
             V((64, 16, 128), BF),
             V((64, 16, 128), F32),
-            dma((3,)),
+            dma((4,)),
         ],
         57,
         6,
@@ -445,7 +431,7 @@
             V((192, 64, 64), BF),
             dma((12,)),
         ],
-        52,
+        49,
         5,
     )(me, near_source.T, inner, vectors, vectors2, outer, near_blocks)
     near_other = lax.ppermute(near_send, "rhs", swap)
@@ -466,16 +452,16 @@
             V((3 * NODES, R, 128), BF),
             dma((5,)),
         ],
-        52,
-        8,
+        49,
+        2,
     )(me, coupling_source.T, inner, msg, outer, raw)
 
     return _call(
         down_kernel,
         "down",
         S((R, 4096), BF),
-        [sm, vm, vm, vm, hbm, hbm, vm, vm],
-        [V((64, R, 128), BF), V((NODES * 64, 128), BF), V(leaf_basis.shape, BF), dma((6,))],
+        [sm] + [vm] * 7,
+        [V((64, R, 128), BF)],
         10,
         4,
     )(me, mine, other, fields, wide, leaf_basis, near_mine, near_other)

time: 79.8 us -> 69.4 us (0.87)
  waiting for transfers between devices: 8.85 us -> 2.36 us
  Pallas kernels: 35.2 us -> 29 us
  starting transfers between devices: 32.4 us -> 36.1 us
  local copies, waits for them, and re-layouts: 2.44 us -> 1.4 us
    all_to_all x1, waiting for transfers between devices: 4.62 us -> 0.01 us  [shards(): lax.all_to_all(send, 'leaf', 0, 0, tiled=True, axis_index_groups=groups)]
    all_to_all x1, starting transfers between devices: 7.44 us -> 11 us  [shards(): lax.all_to_all(partial, 'leaf', 0, 0, tiled=True, axis_index_groups=groups)]
    ppermute x1, starting transfers between devices: 0.1 us -> 3.31 us  [shards(): root2 = lax.ppermute(root, 'leaf', pair)]
    all_to_all x1, waiting for transfers between devices: 3.18 us -> 0.04 us  [shards(): lax.all_to_all(partial, 'leaf', 0, 0, tiled=True, axis_index_groups=groups)]
    pallas_call x1, Pallas kernels: 8.25 us -> 5.52 us  [shards(): _call(field_kernel, 'field', S((64, R, 128), F32), [sm, sm, any_, any_, a...]
    ppermute x3, starting transfers between devices: 4.02 us -> 1.54 us  [the longest x1 1.09 us: shards(): top_target2 = lax.ppermute(target, 'leaf', pair)]
    pallas_call x3, Pallas kernels: 9.71 us -> 7.29 us  [the longest x1 3.49 us: shards(): _call(top_kernel, 'top', (S((NODES * 64, 128), BF), S((128, R, 128), BF))...]
    all_to_all x1, starting transfers between devices: 11.8 us -> 13.3 us  [shards(): lax.all_to_all(send, 'leaf', 0, 0, tiled=True, axis_index_groups=groups)]
  transfers between devices with their start and end apart: 11 -> 11, of which waited for: 4 -> 4; matrix products, arithmetic and copies ran while one was open for 0% -> 0% of each run, Pallas kernels for 39% -> 28%
where the time goes in v3:
time: 69.4 us; the launch traced here: 69.1 us
  starting transfers between devices  36.1 us (52%)
  Pallas kernels  29 us (42%)
  waiting for transfers between devices  2.36 us (3%)
  local copies, waits for them, and re-layouts  1.4 us (2%)
    all_to_all x1, starting transfers between devices, shards(): lax.all_to_all(send, 'leaf', 0, 0, tiled=True, axis_index_groups=groups)  13.3 us
    all_to_all x1, starting transfers between devices, shards(): lax.all_to_all(partial, 'leaf', 0, 0, tiled=True, axis_index_groups=groups)  11 us
    pallas_call x1, Pallas kernels, shards(): _call(field_kernel, 'field', S((64, R, 128), F32), [sm, sm, any_, any_, a...  5.52 us
    pallas_call x1, Pallas kernels, shards(): _call(upper_kernel, 'upper', S((n_leaf // 2, 8, 128), BF), [sm, sm, sm, s...  5.46 us
    pallas_call x1, Pallas kernels, shards(): _call(near_kernel, 'near', (S((R, 4096), F32), S((R, 4096), BF)), [sm, sm...  4.96 us
    pallas_call x1, Pallas kernels, shards(): _call(up_kernel, 'up', (S((128, R, 128), BF), S((R, 128), F32), S((NODES...  4.93 us
    pallas_call x1, Pallas kernels, shards(): _call(top_kernel, 'top', (S((NODES * 64, 128), BF), S((128, R, 128), BF))...  3.49 us
    ppermute x1, starting transfers between devices, shards(): root2 = lax.ppermute(root, 'leaf', pair)  3.31 us
  transfers between devices with their start and end apart: 11, of which 4 were waited for; matrix products, arithmetic and copies ran while one was open for 0% of the time, Pallas kernels for 28%

profile of v3, /device:TPU:1, one launch (start us, length us, event | category | flops | bytes accessed | tf_op | source)
XLA Modules:
  0.0 69.1 jit_solution(14894052625166411214)
XLA Ops:
  0.0 0.0 copy-start.10
  0.0 4.9 %up.1 = (bf16[128,32,128]{2,1,0:T(8,128)(2,1)}, f32[32,128]{1,0:T(8,128)}, bf16[8192,128]{1,0:T(8,128)(2,1)}) custom-call(bf16[32,4096]{1,0:T(8,128)(2,1)} %own_hbm.1, bf16[64,64,64]{2,1,0:T(8,128)(2,1)} %basis_ref.1, bf16[64,64,127]{2,1,0:T(8,128)(2,1)} %bitcast.9), custom_call_target="tpu_custom_call" | custom-call | flops 4000000000 | bytes 12000000 | tf_op jit(solution)/shard_map/up/pallas_call | solution.py:340
  5.0 3.3 %collective-permute-start = (f32[32,128]{1,0:T(8,128)}, f32[32,128]{1,0:T(8,128)S(1)}, u32[]{:S(2)}, u32[]{:S(2)}) collective-permute-start(f32[32,128]{1,0:T(8,128)} %get-tuple-element.17.mine_ref), channel_id=1, source_target_pairs={{0,2},{2,0},{4,6},{6,4},{8,10},{10,8},{12,14},{14,12},{16,18},{18,... | collective-permute-start | bytes 49160 | tf_op jit(solution)/shard_map/ppermute | solution.py:360
  8.3 1.0 %collective-permute-done.other_ref = f32[32,128]{1,0:T(8,128)S(1)} collective-permute-done((f32[32,128]{1,0:T(8,128)}, f32[32,128]{1,0:T(8,128)S(1)}, u32[]{:S(2)}, u32[]{:S(2)}) %collective-permute-start) | collective-permute-done | bytes 16416 | tf_op jit(solution)/shard_map/ppermute | solution.py:360
  9.3 0.7 %copy-done.4 = f32[32,128]{1,0:T(8,128)S(1)} copy-done((f32[32,128]{1,0:T(8,128)S(1)}, f32[32,128]{1,0:T(8,128)}, u32[]{:S(2)}) %copy-start.4) | copy-done | bytes 16408
  10.0 0.7 pack.1.send_hbm
  10.7 0.3 collective-permute-start.3
  11.1 1.2 %collective-permute-start.4 = (bf16[32,4096]{1,0:T(8,128)(2,1)S(1)}, bf16[32,4096]{1,0:T(8,128)(2,1)S(1)}, u32[]{:S(2)}, u32[]{:S(2)}) collective-permute-start(bf16[32,4096]{1,0:T(8,128)(2,1)S(1)} %copy-done.3), channel_id=1, source_target_pairs={{0,1},{1,0},{2,3},{3,2},{4,5},{5,4},{6,7},{7,6},{8,9},{9,8},{10,11... | collective-permute-start | bytes 786440 | tf_op jit(solution)/shard_map/ppermute | solution.py:365
  12.3 13.3 %all-to-all-start = ((bf16[64,8,128]{2,1,0:T(8,128)(2,1)}), bf16[64,8,128]{2,1,0:T(8,128)(2,1)S(1)}, u32[]{:S(2)}, u32[]{:S(2)}) async-start(bf16[64,8,128]{2,1,0:T(8,128)(2,1)} %pack.1.send_hbm), calls=%async_computation | async-start | bytes 262144 | tf_op jit(solution)/shard_map/all_to_all | solution.py:364
  25.5 1.1 %collective-permute-start.1 = (s32[4]{0:T(128)S(1)}, s32[4]{0:T(128)S(1)}, u32[]{:S(2)}, u32[]{:S(2)}) collective-permute-start(s32[4]{0:T(128)S(1)} %copy-done.9), channel_id=1, source_target_pairs={{0,2},{2,0},{4,6},{6,4},{8,10},{10,8},{12,14},{14,12},{16,18},{18,... | collective-permute-start | bytes 56 | tf_op jit(solution)/shard_map/ppermute | solution.py:370
  26.6 0.1 collective-permute-start.2
  26.7 0.7 %collective-permute-done.1.target_hbm.target2_ref = s32[4]{0:T(128)S(1)} collective-permute-done((s32[4]{0:T(128)S(1)}, s32[4]{0:T(128)S(1)}, u32[]{:S(2)}, u32[]{:S(2)}) %collective-permute-start.1) | collective-permute-done | bytes 48 | tf_op jit(solution)/shard_map/ppermute | solution.py:370
  27.5 0.3 collective-permute-done.2.source_hbm.source2_ref
  27.8 0.2 copy-done.11
  28.0 0.3 copy-done.12
  28.3 0.1 copy-done.8
  28.4 3.5 %top.1 = (bf16[8192,128]{1,0:T(8,128)(2,1)}, bf16[128,32,128]{2,1,0:T(8,128)(2,1)}) custom-call(bf16[64,64,126]{2,1,0:T(8,128)(2,1)} %bitcast.10, bf16[128,32,128]{2,1,0:T(8,128)(2,1)} %get-tuple-element.20.msg_hbm, bf16[64,8,128]{2,1,0:T(8,128)(2,1)} %pack.1.send_hbm, bf16[4,64,64]{2,1,0:T(8,128)(2,1)} %copy-done.8, ...), custom_call_target="tpu_custom_call", output_to_operand_aliasing={{1}: (1, {})} | custom-call | flops 4000000000 | bytes 12000000 | tf_op jit(solution)/shard_map/top/pallas_call | solution.py:374
  31.9 0.0 copy-start
  31.9 0.8 %bundle.1.own_hbm = bf16[128,32,128]{2,1,0:T(8,128)(2,1)} custom-call(bf16[128,32,128]{2,1,0:T(8,128)(2,1)} %get-tuple-element.23.msg_ref, bf16[32,4096]{1,0:T(8,128)(2,1)S(1)} %collective-permute-done.4.other_ref.own2_hbm, bf16[64,8,128]{2,1,0:T(8,128)(2,1)S(1)} %all-to-all-done.gathered_ref), custom_call_target="tpu_custom_call", output_to_operand_aliasing={{}: (0, {})} | custom-call | bytes 1000000 | tf_op jit(solution)/shard_map/bundle/pallas_call | solution.py:392
  32.7 2.8 %collective-permute-start.6 = (bf16[128,32,128]{2,1,0:T(8,128)(2,1)}, bf16[128,32,128]{2,1,0:T(8,128)(2,1)S(1)}, u32[]{:S(2)}, u32[]{:S(2)}) collective-permute-start(bf16[128,32,128]{2,1,0:T(8,128)(2,1)} %bundle.1.own_hbm), channel_id=1, source_target_pairs={{2,4},{6,8},{10,12},{14,16},{18,20},{22,24},{26,28},{30,32},{34,36... | collective-permute-start | bytes 3145736 | tf_op jit(solution)/shard_map/ppermute | solution.py:404
  35.5 0.1 collective-permute-start.5
  35.7 5.5 %upper.1 = bf16[64,8,128]{2,1,0:T(8,128)(2,1)} custom-call(s32[4]{0:T(128)} %target_ref.1, s32[4]{0:T(128)} %source_ref.1, s32[4]{0:T(128)} %copy-done.11, s32[4]{0:T(128)} %copy-done.12, bf16[64,8,128]{2,1,0:T(8,128)(2,1)} %copy-done, bf16[8192,128]{1,0:T(8,128)(2,1)} %get-tuple-element.22.wide_hbm, bf16[4,64,64]{2,1,0:T(8,128)(2,1)} %blocks_hbm.2, ...), custom_call_target="tpu_custom_call" | custom-call | flops 6000000000 | bytes 18000000 | tf_op jit(solution)/shard_map/upper/pallas_call | solution.py:405
  41.1 11.0 %all-to-all-start.1 = ((bf16[64,8,128]{2,1,0:T(8,128)(2,1)}), bf16[64,8,128]{2,1,0:T(8,128)(2,1)S(1)}, u32[]{:S(2)}, u32[]{:S(2)}) async-start(bf16[64,8,128]{2,1,0:T(8,128)(2,1)} %upper.1), calls=%async_computation.1 | async-start | bytes 262144 | tf_op jit(solution)/shard_map/all_to_all | solution.py:420
  52.2 0.0 copy-start.1
  52.2 5.0 %near.1 = (f32[32,4096]{1,0:T(8,128)S(1)}, bf16[32,4096]{1,0:T(8,128)(2,1)S(1)}) custom-call(s32[1]{0:T(128)} %bitcast.me_ref, s32[4,64]{1,0:T(4,128)S(1)} %bitcast.7, bf16[128,32,128]{2,1,0:T(8,128)(2,1)S(1)} %collective-permute-done.5.inner_hbm, bf16[32,4096]{1,0:T(8,128)(2,1)S(1)} %copy-done.3, ...), custom_call_target="tpu_custom_call" | custom-call | flops 5000000000 | bytes 15000000 | tf_op jit(solution)/shard_map/near/pallas_call | solution.py:422
  57.1 0.9 %collective-permute-start.8 = (bf16[32,4096]{1,0:T(8,128)(2,1)S(1)}, bf16[32,4096]{1,0:T(8,128)(2,1)S(1)}, u32[]{:S(2)}, u32[]{:S(2)}) collective-permute-start(bf16[32,4096]{1,0:T(8,128)(2,1)S(1)} %get-tuple-element.28), channel_id=1, source_target_pairs={{0,1},{1,0},{2,3},{3,2},{4,5},{5,4},{6,7},{7,6},{8,9},{9,8},{10,11... | collective-permute-start | bytes 786440 | tf_op jit(solution)/shard_map/ppermute | solution.py:437
  58.0 0.0 all-to-all-done.1.parts_ref
  58.0 0.1 total.1.mine_ref
  58.1 2.0 %collective-permute-start.7 = (f32[8,128]{1,0:T(8,128)S(1)}, f32[8,128]{1,0:T(8,128)S(1)}, u32[]{:S(2)}, u32[]{:S(2)}) collective-permute-start(f32[8,128]{1,0:T(8,128)S(1)} %total.1.mine_ref), channel_id=1, source_target_pairs={{0,2},{2,0},{4,6},{6,4},{8,10},{10,8},{12,14},{14,12},{16,18},{18,... | collective-permute-start | bytes 12296 | tf_op jit(solution)/shard_map/ppermute | solution.py:440
  60.1 5.5 %field.1.field_ref = f32[64,32,128]{2,1,0:T(8,128)S(1)} custom-call(s32[1]{0:T(128)} %bitcast.me_ref, s32[4,127]{1,0:T(4,128)S(1)} %bitcast.6, bf16[128,32,128]{2,1,0:T(8,128)(2,1)S(1)} %collective-permute-done.5.inner_hbm, bf16[128,32,128]{2,1,0:T(8,128)(2,1)} %bundle.1.own_hbm, bf16[128,32,128]{2,1,0:T(8,128)(2,1)S(1)} %collective-permute-done.6.outer_hbm, ...), custom_call_target="tpu_custom_call" | custom-call | flops 2000000000 | bytes 6000000 | tf_op jit(solution)/shard_map/field/pallas_call | solution.py:443
  65.7 0.2 collective-permute-done.8.near2_ref
  65.9 3.1 %down.1 = bf16[32,4096]{1,0:T(8,128)(2,1)} custom-call(s32[1]{0:T(128)} %bitcast.me_ref, f32[8,128]{1,0:T(8,128)S(1)} %total.1.mine_ref, f32[8,128]{1,0:T(8,128)S(1)} %collective-permute-done.7.other_ref, f32[64,32,128]{2,1,0:T(8,128)S(1)} %field.1.field_ref, bf16[8192,128]{1,0:T(8,128)(2,1)S(1)} %copy-done.6, bf16[64,64,64]{2,1,0:T(8,128)(2,1)S(1)} %copy-done.2, ...), custom_call_target="tpu_custom_call" | custom-call | flops 4000000000 | bytes 12000000 | tf_op jit(solution)/shard_map/down/pallas_call | solution.py:459
  (25 shorter events, 0.1 us)
Async XLA Ops:
  0.0 10.7 %copy-start.7 = (bf16[4,64,64]{2,1,0:T(8,128)(2,1)S(1)}, bf16[4,64,64]{2,1,0:T(8,128)(2,1)}, u32[]{:S(2)}) copy-start(bf16[4,64,64]{2,1,0:T(8,128)(2,1)} %blocks_hbm.2) | copy-start | bytes 98308
  0.0 11.1 %copy-start.3 = (bf16[32,4096]{1,0:T(8,128)(2,1)S(1)}, bf16[32,4096]{1,0:T(8,128)(2,1)}, u32[]{:S(2)}) copy-start(bf16[32,4096]{1,0:T(8,128)(2,1)} %own_hbm.1) | copy-start | bytes 786436
  0.0 25.5 %copy-start.9 = (s32[4]{0:T(128)S(1)}, s32[4]{0:T(128)}, u32[]{:S(2)}) copy-start(s32[4]{0:T(128)} %target_ref.1) | copy-start | bytes 52
  0.0 26.6 %copy-start.10 = (s32[4]{0:T(128)S(1)}, s32[4]{0:T(128)}, u32[]{:S(2)}) copy-start(s32[4]{0:T(128)} %source_ref.1) | copy-start | bytes 52
  5.0 4.4 %collective-permute-start = (f32[32,128]{1,0:T(8,128)}, f32[32,128]{1,0:T(8,128)S(1)}, u32[]{:S(2)}, u32[]{:S(2)}) collective-permute-start(f32[32,128]{1,0:T(8,128)} %get-tuple-element.17.mine_ref), channel_id=1, source_target_pairs={{0,2},{2,0},{4,6},{6,4},{8,10},{10,8},{12,14},{14,12},{16,18},{18,... | collective-permute-start | bytes 49160 | tf_op jit(solution)/shard_map/ppermute | solution.py:360
  9.3 0.7 %copy-start.4 = (f32[32,128]{1,0:T(8,128)S(1)}, f32[32,128]{1,0:T(8,128)}, u32[]{:S(2)}) copy-start(f32[32,128]{1,0:T(8,128)} %get-tuple-element.17.mine_ref) | copy-start | bytes 49156
  10.7 17.1 %collective-permute-start.3 = (bf16[4,64,64]{2,1,0:T(8,128)(2,1)S(1)}, bf16[4,64,64]{2,1,0:T(8,128)(2,1)S(1)}, u32[]{:S(2)}, u32[]{:S(2)}) collective-permute-start(bf16[4,64,64]{2,1,0:T(8,128)(2,1)S(1)} %copy-done.7), channel_id=1, source_target_pairs={{0,2},{2,0},{4,6},{6,4},{8,10},{10,8},{12,14},{14,12},{16,18},{18,... | collective-permute-start | bytes 98312 | tf_op jit(solution)/shard_map/ppermute | solution.py:369
  11.1 20.8 %collective-permute-start.4 = (bf16[32,4096]{1,0:T(8,128)(2,1)S(1)}, bf16[32,4096]{1,0:T(8,128)(2,1)S(1)}, u32[]{:S(2)}, u32[]{:S(2)}) collective-permute-start(bf16[32,4096]{1,0:T(8,128)(2,1)S(1)} %copy-done.3), channel_id=1, source_target_pairs={{0,1},{1,0},{2,3},{3,2},{4,5},{5,4},{6,7},{7,6},{8,9},{9,8},{10,11... | collective-permute-start | bytes 786440 | tf_op jit(solution)/shard_map/ppermute | solution.py:365
  12.3 19.7 %all-to-all-start = ((bf16[64,8,128]{2,1,0:T(8,128)(2,1)}), bf16[64,8,128]{2,1,0:T(8,128)(2,1)S(1)}, u32[]{:S(2)}, u32[]{:S(2)}) async-start(bf16[64,8,128]{2,1,0:T(8,128)(2,1)} %pack.1.send_hbm), calls=%async_computation | async-start | bytes 262144 | tf_op jit(solution)/shard_map/all_to_all | solution.py:364
  25.5 1.9 %collective-permute-start.1 = (s32[4]{0:T(128)S(1)}, s32[4]{0:T(128)S(1)}, u32[]{:S(2)}, u32[]{:S(2)}) collective-permute-start(s32[4]{0:T(128)S(1)} %copy-done.9), channel_id=1, source_target_pairs={{0,2},{2,0},{4,6},{6,4},{8,10},{10,8},{12,14},{14,12},{16,18},{18,... | collective-permute-start | bytes 56 | tf_op jit(solution)/shard_map/ppermute | solution.py:370
  26.6 1.1 %collective-permute-start.2 = (s32[4]{0:T(128)S(1)}, s32[4]{0:T(128)S(1)}, u32[]{:S(2)}, u32[]{:S(2)}) collective-permute-start(s32[4]{0:T(128)S(1)} %copy-done.10), channel_id=1, source_target_pairs={{0,2},{2,0},{4,6},{6,4},{8,10},{10,8},{12,14},{14,12},{16,18},{18,... | collective-permute-start | bytes 56 | tf_op jit(solution)/shard_map/ppermute | solution.py:371
  27.5 0.5 copy-start.11
  27.8 0.5 copy-start.12
  27.8 0.6 copy-start.8
  31.9 3.7 %copy-start = (bf16[64,8,128]{2,1,0:T(8,128)(2,1)}, bf16[64,8,128]{2,1,0:T(8,128)(2,1)S(1)}, u32[]{:S(2)}) copy-start(bf16[64,8,128]{2,1,0:T(8,128)(2,1)S(1)} %all-to-all-done.gathered_ref) | copy-start | bytes 393220
  32.7 19.4 %collective-permute-start.6 = (bf16[128,32,128]{2,1,0:T(8,128)(2,1)}, bf16[128,32,128]{2,1,0:T(8,128)(2,1)S(1)}, u32[]{:S(2)}, u32[]{:S(2)}) collective-permute-start(bf16[128,32,128]{2,1,0:T(8,128)(2,1)} %bundle.1.own_hbm), channel_id=1, source_target_pairs={{2,4},{6,8},{10,12},{14,16},{18,20},{22,24},{26,28},{30,32},{34,36... | collective-permute-start | bytes 3145736 | tf_op jit(solution)/shard_map/ppermute | solution.py:404
  35.5 16.6 %collective-permute-start.5 = (bf16[128,32,128]{2,1,0:T(8,128)(2,1)}, bf16[128,32,128]{2,1,0:T(8,128)(2,1)S(1)}, u32[]{:S(2)}, u32[]{:S(2)}) collective-permute-start(bf16[128,32,128]{2,1,0:T(8,128)(2,1)} %bundle.1.own_hbm), channel_id=1, source_target_pairs={{0,2},{2,0},{4,6},{6,4},{8,10},{10,8},{12,14},{14,12},{16,18},{18,... | collective-permute-start | bytes 3145736 | tf_op jit(solution)/shard_map/ppermute | solution.py:403
  35.6 16.5 %copy-start.5 = (s32[64,4]{0,1:T(4,128)S(1)}, s32[64,4]{0,1:T(4,128)}, u32[]{:S(2)}) copy-start(s32[64,4]{0,1:T(4,128)} %param.21) | copy-start | bytes 3076
  41.1 16.9 %all-to-all-start.1 = ((bf16[64,8,128]{2,1,0:T(8,128)(2,1)}), bf16[64,8,128]{2,1,0:T(8,128)(2,1)S(1)}, u32[]{:S(2)}, u32[]{:S(2)}) async-start(bf16[64,8,128]{2,1,0:T(8,128)(2,1)} %upper.1), calls=%async_computation.1 | async-start | bytes 262144 | tf_op jit(solution)/shard_map/all_to_all | solution.py:420
  52.2 8.0 %copy-start.1 = (s32[127,4]{0,1:T(4,128)S(1)}, s32[127,4]{0,1:T(4,128)}, u32[]{:S(2)}) copy-start(s32[127,4]{0,1:T(4,128)} %param.15) | copy-start | bytes 6100
  57.1 8.8 %collective-permute-start.8 = (bf16[32,4096]{1,0:T(8,128)(2,1)S(1)}, bf16[32,4096]{1,0:T(8,128)(2,1)S(1)}, u32[]{:S(2)}, u32[]{:S(2)}) collective-permute-start(bf16[32,4096]{1,0:T(8,128)(2,1)S(1)} %get-tuple-element.28), channel_id=1, source_target_pairs={{0,1},{1,0},{2,3},{3,2},{4,5},{5,4},{6,7},{7,6},{8,9},{9,8},{10,11... | collective-permute-start | bytes 786440 | tf_op jit(solution)/shard_map/ppermute | solution.py:437
  58.1 7.6 %collective-permute-start.7 = (f32[8,128]{1,0:T(8,128)S(1)}, f32[8,128]{1,0:T(8,128)S(1)}, u32[]{:S(2)}, u32[]{:S(2)}) collective-permute-start(f32[8,128]{1,0:T(8,128)S(1)} %total.1.mine_ref), channel_id=1, source_target_pairs={{0,2},{2,0},{4,6},{6,4},{8,10},{10,8},{12,14},{14,12},{16,18},{18,... | collective-permute-start | bytes 12296 | tf_op jit(solution)/shard_map/ppermute | solution.py:440
  60.1 5.8 %copy-start.2 = (bf16[64,64,64]{2,1,0:T(8,128)(2,1)S(1)}, bf16[64,64,64]{2,1,0:T(8,128)(2,1)}, u32[]{:S(2)}) copy-start(bf16[64,64,64]{2,1,0:T(8,128)(2,1)} %basis_ref.1) | copy-start | bytes 1572868
  60.1 5.8 %copy-start.6 = (bf16[8192,128]{1,0:T(8,128)(2,1)S(1)}, bf16[8192,128]{1,0:T(8,128)(2,1)}, u32[]{:S(2)}) copy-start(bf16[8192,128]{1,0:T(8,128)(2,1)} %get-tuple-element.26.wide_ref) | copy-start | bytes 6291460

commit v4 on v3

--- a/solution.py
+++ b/solution.py
@@ -54,9 +54,10 @@
     ]
 
 
-def _unstack(raw_ref, wide, copy):
-    copy.wait()
+def _unstack(raw_ref, wide, copies):
     for k in range(64):
+        if k % 32 == 0:
+            copies[k // 32].wait()
         block = raw_ref[k].astype(F32)
         both = jnp.concatenate([block, block], axis=0)
         wide[pl.ds(k, raw_ref.shape[2], stride=PITCH), :] = both.T
@@ -70,14 +71,14 @@
 def up_kernel(
     v_hbm, basis_hbm, raw_hbm, msg_hbm, root_ref, wide_hbm, v_ref, basis_ref, raw_ref, msg_ref, wide, wide_ref, sems, out_sems
 ):
-    copies = _fetch(sems, (raw_hbm, raw_ref), (v_hbm, v_ref), (basis_hbm, basis_ref))
+    copies = _fetch(sems, *_chunks(raw_hbm, raw_ref, 2), (v_hbm, v_ref), (basis_hbm, basis_ref))
     low = _low(R)
     zero = jnp.zeros((R, 128), BF)
-    _unstack(raw_ref, wide, copies[0])
+    _unstack(raw_ref, wide, copies)
     _narrow(wide, wide_ref, raw_ref.shape[2])
     out = _fetch(out_sems, (wide_ref, wide_hbm))
-    copies[1].wait()
     copies[2].wait()
+    copies[3].wait()
     for p in range(32):
         v = v_ref[:, 128 * p : 128 * p + 128]
         msg_ref[64 + p] = v
@@ -119,8 +120,8 @@
 
 
 def top_kernel(raw_hbm, msg_hbm, send_hbm, block_hbm, target_hbm, source_hbm, wide_hbm, msg_out, raw_ref, wide, wide_ref, sems, out_sems):
-    copies = _fetch(sems, (raw_hbm, raw_ref))
-    _unstack(raw_ref, wide, copies[0])
+    copies = _fetch(sems, *_chunks(raw_hbm, raw_ref, 2))
+    _unstack(raw_ref, wide, copies)
     _narrow(wide, wide_ref, raw_ref.shape[2])
     out = _fetch(out_sems, (wide_ref, wide_hbm))
     out[0].wait()
@@ -349,7 +350,7 @@
             V((96, R, 128), BF),
             V((NODES * PITCH, 128), F32),
             V((NODES * 64, 128), BF),
-            dma((3,)),
+            dma((4,)),
             dma((4,)),
         ],
         59,
@@ -380,7 +381,7 @@
             V(raw.shape, BF),
             V((NODES * PITCH, 128), F32),
             V((NODES * 64, 128), BF),
-            dma((1,)),
+            dma((2,)),
             dma((1,)),
         ],
         57,

time: 69.4 us -> 69 us (level)
  no operation moved by 1% of the time
where the time goes in v4:
time: 69 us; the launch traced here: 68.7 us
  starting transfers between devices  36.2 us (52%)
  Pallas kernels  28.7 us (42%)
  waiting for transfers between devices  2.26 us (3%)
  local copies, waits for them, and re-layouts  1.4 us (2%)
    all_to_all x1, starting transfers between devices, shards(): lax.all_to_all(send, 'leaf', 0, 0, tiled=True, axis_index_groups=groups)  13.3 us
    all_to_all x1, starting transfers between devices, shards(): lax.all_to_all(partial, 'leaf', 0, 0, tiled=True, axis_index_groups=groups)  10.9 us
    pallas_call x1, Pallas kernels, shards(): _call(field_kernel, 'field', S((64, R, 128), F32), [sm, sm, any_, any_, a...  5.51 us
    pallas_call x1, Pallas kernels, shards(): _call(upper_kernel, 'upper', S((n_leaf // 2, 8, 128), BF), [sm, sm, sm, s...  5.47 us
    pallas_call x1, Pallas kernels, shards(): _call(near_kernel, 'near', (S((R, 4096), F32), S((R, 4096), BF)), [sm, sm...  4.96 us
    pallas_call x1, Pallas kernels, shards(): _call(up_kernel, 'up', (S((128, R, 128), BF), S((R, 128), F32), S((NODES...  4.76 us
    pallas_call x1, Pallas kernels, shards(): _call(top_kernel, 'top', (S((NODES * 64, 128), BF), S((128, R, 128), BF))...  3.32 us
    ppermute x1, starting transfers between devices, shards(): root2 = lax.ppermute(root, 'leaf', pair)  3.31 us
  transfers between devices with their start and end apart: 11, of which 4 were waited for; matrix products, arithmetic and copies ran while one was open for 0% of the time, Pallas kernels for 28%

profile of v4, /device:TPU:1, one launch (start us, length us, event | category | flops | bytes accessed | tf_op | source)
XLA Modules:
  0.0 68.7 jit_solution(8200371575590706882)
XLA Ops:
  0.0 0.0 copy-start.10
  0.0 4.8 %up.1 = (bf16[128,32,128]{2,1,0:T(8,128)(2,1)}, f32[32,128]{1,0:T(8,128)}, bf16[8192,128]{1,0:T(8,128)(2,1)}) custom-call(bf16[32,4096]{1,0:T(8,128)(2,1)} %own_hbm.1, bf16[64,64,64]{2,1,0:T(8,128)(2,1)} %basis_ref.1, bf16[64,64,127]{2,1,0:T(8,128)(2,1)} %bitcast.9), custom_call_target="tpu_custom_call" | custom-call | flops 4000000000 | bytes 12000000 | tf_op jit(solution)/shard_map/up/pallas_call | solution.py:341
  4.8 3.3 %collective-permute-start = (f32[32,128]{1,0:T(8,128)}, f32[32,128]{1,0:T(8,128)S(1)}, u32[]{:S(2)}, u32[]{:S(2)}) collective-permute-start(f32[32,128]{1,0:T(8,128)} %get-tuple-element.17.mine_ref), channel_id=1, source_target_pairs={{0,2},{2,0},{4,6},{6,4},{8,10},{10,8},{12,14},{14,12},{16,18},{18,... | collective-permute-start | bytes 49160 | tf_op jit(solution)/shard_map/ppermute | solution.py:361
  8.1 1.0 %collective-permute-done.other_ref = f32[32,128]{1,0:T(8,128)S(1)} collective-permute-done((f32[32,128]{1,0:T(8,128)}, f32[32,128]{1,0:T(8,128)S(1)}, u32[]{:S(2)}, u32[]{:S(2)}) %collective-permute-start) | collective-permute-done | bytes 16416 | tf_op jit(solution)/shard_map/ppermute | solution.py:361
  9.2 0.7 %copy-done.4 = f32[32,128]{1,0:T(8,128)S(1)} copy-done((f32[32,128]{1,0:T(8,128)S(1)}, f32[32,128]{1,0:T(8,128)}, u32[]{:S(2)}) %copy-start.4) | copy-done | bytes 16408
  9.9 0.7 pack.1.send_hbm
  10.5 0.3 collective-permute-start.3
  10.9 1.2 %collective-permute-start.4 = (bf16[32,4096]{1,0:T(8,128)(2,1)S(1)}, bf16[32,4096]{1,0:T(8,128)(2,1)S(1)}, u32[]{:S(2)}, u32[]{:S(2)}) collective-permute-start(bf16[32,4096]{1,0:T(8,128)(2,1)S(1)} %copy-done.3), channel_id=1, source_target_pairs={{0,1},{1,0},{2,3},{3,2},{4,5},{5,4},{6,7},{7,6},{8,9},{9,8},{10,11... | collective-permute-start | bytes 786440 | tf_op jit(solution)/shard_map/ppermute | solution.py:366
  12.1 13.3 %all-to-all-start = ((bf16[64,8,128]{2,1,0:T(8,128)(2,1)}), bf16[64,8,128]{2,1,0:T(8,128)(2,1)S(1)}, u32[]{:S(2)}, u32[]{:S(2)}) async-start(bf16[64,8,128]{2,1,0:T(8,128)(2,1)} %pack.1.send_hbm), calls=%async_computation | async-start | bytes 262144 | tf_op jit(solution)/shard_map/all_to_all | solution.py:365
  25.4 1.1 %collective-permute-start.1 = (s32[4]{0:T(128)S(1)}, s32[4]{0:T(128)S(1)}, u32[]{:S(2)}, u32[]{:S(2)}) collective-permute-start(s32[4]{0:T(128)S(1)} %copy-done.9), channel_id=1, source_target_pairs={{0,2},{2,0},{4,6},{6,4},{8,10},{10,8},{12,14},{14,12},{16,18},{18,... | collective-permute-start | bytes 56 | tf_op jit(solution)/shard_map/ppermute | solution.py:371
  26.5 0.1 collective-permute-start.2
  26.6 0.7 %collective-permute-done.1.target_hbm.target2_ref = s32[4]{0:T(128)S(1)} collective-permute-done((s32[4]{0:T(128)S(1)}, s32[4]{0:T(128)S(1)}, u32[]{:S(2)}, u32[]{:S(2)}) %collective-permute-start.1) | collective-permute-done | bytes 48 | tf_op jit(solution)/shard_map/ppermute | solution.py:371
  27.3 0.3 collective-permute-done.2.source_hbm.source2_ref
  27.6 0.2 copy-done.11
  27.8 0.3 copy-done.12
  28.1 0.1 copy-done.8
  28.2 3.3 %top.1 = (bf16[8192,128]{1,0:T(8,128)(2,1)}, bf16[128,32,128]{2,1,0:T(8,128)(2,1)}) custom-call(bf16[64,64,126]{2,1,0:T(8,128)(2,1)} %bitcast.10, bf16[128,32,128]{2,1,0:T(8,128)(2,1)} %get-tuple-element.20.msg_hbm, bf16[64,8,128]{2,1,0:T(8,128)(2,1)} %pack.1.send_hbm, bf16[4,64,64]{2,1,0:T(8,128)(2,1)} %copy-done.8, ...), custom_call_target="tpu_custom_call", output_to_operand_aliasing={{1}: (1, {})} | custom-call | flops 4000000000 | bytes 12000000 | tf_op jit(solution)/shard_map/top/pallas_call | solution.py:375
  31.6 0.0 copy-start
  31.6 0.8 %bundle.1.own_hbm = bf16[128,32,128]{2,1,0:T(8,128)(2,1)} custom-call(bf16[128,32,128]{2,1,0:T(8,128)(2,1)} %get-tuple-element.23.msg_ref, bf16[32,4096]{1,0:T(8,128)(2,1)S(1)} %collective-permute-done.4.other_ref.own2_hbm, bf16[64,8,128]{2,1,0:T(8,128)(2,1)S(1)} %all-to-all-done.gathered_ref), custom_call_target="tpu_custom_call", output_to_operand_aliasing={{}: (0, {})} | custom-call | bytes 1000000 | tf_op jit(solution)/shard_map/bundle/pallas_call | solution.py:393
  32.4 3.0 %collective-permute-start.6 = (bf16[128,32,128]{2,1,0:T(8,128)(2,1)}, bf16[128,32,128]{2,1,0:T(8,128)(2,1)S(1)}, u32[]{:S(2)}, u32[]{:S(2)}) collective-permute-start(bf16[128,32,128]{2,1,0:T(8,128)(2,1)} %bundle.1.own_hbm), channel_id=1, source_target_pairs={{2,4},{6,8},{10,12},{14,16},{18,20},{22,24},{26,28},{30,32},{34,36... | collective-permute-start | bytes 3145736 | tf_op jit(solution)/shard_map/ppermute | solution.py:405
  35.4 0.1 collective-permute-start.5
  35.5 5.5 %upper.1 = bf16[64,8,128]{2,1,0:T(8,128)(2,1)} custom-call(s32[4]{0:T(128)} %target_ref.1, s32[4]{0:T(128)} %source_ref.1, s32[4]{0:T(128)} %copy-done.11, s32[4]{0:T(128)} %copy-done.12, bf16[64,8,128]{2,1,0:T(8,128)(2,1)} %copy-done, bf16[8192,128]{1,0:T(8,128)(2,1)} %get-tuple-element.22.wide_hbm, bf16[4,64,64]{2,1,0:T(8,128)(2,1)} %blocks_hbm.2, ...), custom_call_target="tpu_custom_call" | custom-call | flops 6000000000 | bytes 18000000 | tf_op jit(solution)/shard_map/upper/pallas_call | solution.py:406
  41.0 10.9 %all-to-all-start.1 = ((bf16[64,8,128]{2,1,0:T(8,128)(2,1)}), bf16[64,8,128]{2,1,0:T(8,128)(2,1)S(1)}, u32[]{:S(2)}, u32[]{:S(2)}) async-start(bf16[64,8,128]{2,1,0:T(8,128)(2,1)} %upper.1), calls=%async_computation.1 | async-start | bytes 262144 | tf_op jit(solution)/shard_map/all_to_all | solution.py:421
  51.9 0.0 copy-start.1
  51.9 5.0 %near.1 = (f32[32,4096]{1,0:T(8,128)S(1)}, bf16[32,4096]{1,0:T(8,128)(2,1)S(1)}) custom-call(s32[1]{0:T(128)} %bitcast.me_ref, s32[4,64]{1,0:T(4,128)S(1)} %bitcast.7, bf16[128,32,128]{2,1,0:T(8,128)(2,1)S(1)} %collective-permute-done.5.inner_hbm, bf16[32,4096]{1,0:T(8,128)(2,1)S(1)} %copy-done.3, ...), custom_call_target="tpu_custom_call" | custom-call | flops 5000000000 | bytes 15000000 | tf_op jit(solution)/shard_map/near/pallas_call | solution.py:423
  56.9 0.9 %collective-permute-start.8 = (bf16[32,4096]{1,0:T(8,128)(2,1)S(1)}, bf16[32,4096]{1,0:T(8,128)(2,1)S(1)}, u32[]{:S(2)}, u32[]{:S(2)}) collective-permute-start(bf16[32,4096]{1,0:T(8,128)(2,1)S(1)} %get-tuple-element.28), channel_id=1, source_target_pairs={{0,1},{1,0},{2,3},{3,2},{4,5},{5,4},{6,7},{7,6},{8,9},{9,8},{10,11... | collective-permute-start | bytes 786440 | tf_op jit(solution)/shard_map/ppermute | solution.py:438
  57.7 0.0 all-to-all-done.1.parts_ref
  57.8 0.1 total.1.mine_ref
  57.9 2.0 %collective-permute-start.7 = (f32[8,128]{1,0:T(8,128)S(1)}, f32[8,128]{1,0:T(8,128)S(1)}, u32[]{:S(2)}, u32[]{:S(2)}) collective-permute-start(f32[8,128]{1,0:T(8,128)S(1)} %total.1.mine_ref), channel_id=1, source_target_pairs={{0,2},{2,0},{4,6},{6,4},{8,10},{10,8},{12,14},{14,12},{16,18},{18,... | collective-permute-start | bytes 12296 | tf_op jit(solution)/shard_map/ppermute | solution.py:441
  59.9 5.5 %field.1.field_ref = f32[64,32,128]{2,1,0:T(8,128)S(1)} custom-call(s32[1]{0:T(128)} %bitcast.me_ref, s32[4,127]{1,0:T(4,128)S(1)} %bitcast.6, bf16[128,32,128]{2,1,0:T(8,128)(2,1)S(1)} %collective-permute-done.5.inner_hbm, bf16[128,32,128]{2,1,0:T(8,128)(2,1)} %bundle.1.own_hbm, bf16[128,32,128]{2,1,0:T(8,128)(2,1)S(1)} %collective-permute-done.6.outer_hbm, ...), custom_call_target="tpu_custom_call" | custom-call | flops 2000000000 | bytes 6000000 | tf_op jit(solution)/shard_map/field/pallas_call | solution.py:444
  65.4 0.1 collective-permute-done.8.near2_ref
  65.5 3.1 %down.1 = bf16[32,4096]{1,0:T(8,128)(2,1)} custom-call(s32[1]{0:T(128)} %bitcast.me_ref, f32[8,128]{1,0:T(8,128)S(1)} %total.1.mine_ref, f32[8,128]{1,0:T(8,128)S(1)} %collective-permute-done.7.other_ref, f32[64,32,128]{2,1,0:T(8,128)S(1)} %field.1.field_ref, bf16[8192,128]{1,0:T(8,128)(2,1)S(1)} %copy-done.6, bf16[64,64,64]{2,1,0:T(8,128)(2,1)S(1)} %copy-done.2, ...), custom_call_target="tpu_custom_call" | custom-call | flops 4000000000 | bytes 12000000 | tf_op jit(solution)/shard_map/down/pallas_call | solution.py:460
  (25 shorter events, 0.1 us)
Async XLA Ops:
  0.0 10.5 %copy-start.7 = (bf16[4,64,64]{2,1,0:T(8,128)(2,1)S(1)}, bf16[4,64,64]{2,1,0:T(8,128)(2,1)}, u32[]{:S(2)}) copy-start(bf16[4,64,64]{2,1,0:T(8,128)(2,1)} %blocks_hbm.2) | copy-start | bytes 98308
  0.0 10.9 %copy-start.3 = (bf16[32,4096]{1,0:T(8,128)(2,1)S(1)}, bf16[32,4096]{1,0:T(8,128)(2,1)}, u32[]{:S(2)}) copy-start(bf16[32,4096]{1,0:T(8,128)(2,1)} %own_hbm.1) | copy-start | bytes 786436
  0.0 25.4 %copy-start.9 = (s32[4]{0:T(128)S(1)}, s32[4]{0:T(128)}, u32[]{:S(2)}) copy-start(s32[4]{0:T(128)} %target_ref.1) | copy-start | bytes 52
  0.0 26.5 %copy-start.10 = (s32[4]{0:T(128)S(1)}, s32[4]{0:T(128)}, u32[]{:S(2)}) copy-start(s32[4]{0:T(128)} %source_ref.1) | copy-start | bytes 52
  4.8 4.4 %collective-permute-start = (f32[32,128]{1,0:T(8,128)}, f32[32,128]{1,0:T(8,128)S(1)}, u32[]{:S(2)}, u32[]{:S(2)}) collective-permute-start(f32[32,128]{1,0:T(8,128)} %get-tuple-element.17.mine_ref), channel_id=1, source_target_pairs={{0,2},{2,0},{4,6},{6,4},{8,10},{10,8},{12,14},{14,12},{16,18},{18,... | collective-permute-start | bytes 49160 | tf_op jit(solution)/shard_map/ppermute | solution.py:361
  9.2 0.7 %copy-start.4 = (f32[32,128]{1,0:T(8,128)S(1)}, f32[32,128]{1,0:T(8,128)}, u32[]{:S(2)}) copy-start(f32[32,128]{1,0:T(8,128)} %get-tuple-element.17.mine_ref) | copy-start | bytes 49156
  10.5 17.1 %collective-permute-start.3 = (bf16[4,64,64]{2,1,0:T(8,128)(2,1)S(1)}, bf16[4,64,64]{2,1,0:T(8,128)(2,1)S(1)}, u32[]{:S(2)}, u32[]{:S(2)}) collective-permute-start(bf16[4,64,64]{2,1,0:T(8,128)(2,1)S(1)} %copy-done.7), channel_id=1, source_target_pairs={{0,2},{2,0},{4,6},{6,4},{8,10},{10,8},{12,14},{14,12},{16,18},{18,... | collective-permute-start | bytes 98312 | tf_op jit(solution)/shard_map/ppermute | solution.py:370
  10.9 20.7 %collective-permute-start.4 = (bf16[32,4096]{1,0:T(8,128)(2,1)S(1)}, bf16[32,4096]{1,0:T(8,128)(2,1)S(1)}, u32[]{:S(2)}, u32[]{:S(2)}) collective-permute-start(bf16[32,4096]{1,0:T(8,128)(2,1)S(1)} %copy-done.3), channel_id=1, source_target_pairs={{0,1},{1,0},{2,3},{3,2},{4,5},{5,4},{6,7},{7,6},{8,9},{9,8},{10,11... | collective-permute-start | bytes 786440 | tf_op jit(solution)/shard_map/ppermute | solution.py:366
  12.1 19.5 %all-to-all-start = ((bf16[64,8,128]{2,1,0:T(8,128)(2,1)}), bf16[64,8,128]{2,1,0:T(8,128)(2,1)S(1)}, u32[]{:S(2)}, u32[]{:S(2)}) async-start(bf16[64,8,128]{2,1,0:T(8,128)(2,1)} %pack.1.send_hbm), calls=%async_computation | async-start | bytes 262144 | tf_op jit(solution)/shard_map/all_to_all | solution.py:365
  25.4 1.9 %collective-permute-start.1 = (s32[4]{0:T(128)S(1)}, s32[4]{0:T(128)S(1)}, u32[]{:S(2)}, u32[]{:S(2)}) collective-permute-start(s32[4]{0:T(128)S(1)} %copy-done.9), channel_id=1, source_target_pairs={{0,2},{2,0},{4,6},{6,4},{8,10},{10,8},{12,14},{14,12},{16,18},{18,... | collective-permute-start | bytes 56 | tf_op jit(solution)/shard_map/ppermute | solution.py:371
  26.5 1.1 %collective-permute-start.2 = (s32[4]{0:T(128)S(1)}, s32[4]{0:T(128)S(1)}, u32[]{:S(2)}, u32[]{:S(2)}) collective-permute-start(s32[4]{0:T(128)S(1)} %copy-done.10), channel_id=1, source_target_pairs={{0,2},{2,0},{4,6},{6,4},{8,10},{10,8},{12,14},{14,12},{16,18},{18,... | collective-permute-start | bytes 56 | tf_op jit(solution)/shard_map/ppermute | solution.py:372
  27.3 0.5 copy-start.11
  27.6 0.5 copy-start.12
  27.6 0.6 copy-start.8
  31.6 3.9 %copy-start = (bf16[64,8,128]{2,1,0:T(8,128)(2,1)}, bf16[64,8,128]{2,1,0:T(8,128)(2,1)S(1)}, u32[]{:S(2)}) copy-start(bf16[64,8,128]{2,1,0:T(8,128)(2,1)S(1)} %all-to-all-done.gathered_ref) | copy-start | bytes 393220
  32.4 19.5 %collective-permute-start.6 = (bf16[128,32,128]{2,1,0:T(8,128)(2,1)}, bf16[128,32,128]{2,1,0:T(8,128)(2,1)S(1)}, u32[]{:S(2)}, u32[]{:S(2)}) collective-permute-start(bf16[128,32,128]{2,1,0:T(8,128)(2,1)} %bundle.1.own_hbm), channel_id=1, source_target_pairs={{2,4},{6,8},{10,12},{14,16},{18,20},{22,24},{26,28},{30,32},{34,36... | collective-permute-start | bytes 3145736 | tf_op jit(solution)/shard_map/ppermute | solution.py:405
  35.4 16.5 %collective-permute-start.5 = (bf16[128,32,128]{2,1,0:T(8,128)(2,1)}, bf16[128,32,128]{2,1,0:T(8,128)(2,1)S(1)}, u32[]{:S(2)}, u32[]{:S(2)}) collective-permute-start(bf16[128,32,128]{2,1,0:T(8,128)(2,1)} %bundle.1.own_hbm), channel_id=1, source_target_pairs={{0,2},{2,0},{4,6},{6,4},{8,10},{10,8},{12,14},{14,12},{16,18},{18,... | collective-permute-start | bytes 3145736 | tf_op jit(solution)/shard_map/ppermute | solution.py:404
  35.5 16.4 %copy-start.5 = (s32[64,4]{0,1:T(4,128)S(1)}, s32[64,4]{0,1:T(4,128)}, u32[]{:S(2)}) copy-start(s32[64,4]{0,1:T(4,128)} %param.21) | copy-start | bytes 3076
  41.0 16.8 %all-to-all-start.1 = ((bf16[64,8,128]{2,1,0:T(8,128)(2,1)}), bf16[64,8,128]{2,1,0:T(8,128)(2,1)S(1)}, u32[]{:S(2)}, u32[]{:S(2)}) async-start(bf16[64,8,128]{2,1,0:T(8,128)(2,1)} %upper.1), calls=%async_computation.1 | async-start | bytes 262144 | tf_op jit(solution)/shard_map/all_to_all | solution.py:421
  51.9 8.0 %copy-start.1 = (s32[127,4]{0,1:T(4,128)S(1)}, s32[127,4]{0,1:T(4,128)}, u32[]{:S(2)}) copy-start(s32[127,4]{0,1:T(4,128)} %param.15) | copy-start | bytes 6100
  56.9 8.7 %collective-permute-start.8 = (bf16[32,4096]{1,0:T(8,128)(2,1)S(1)}, bf16[32,4096]{1,0:T(8,128)(2,1)S(1)}, u32[]{:S(2)}, u32[]{:S(2)}) collective-permute-start(bf16[32,4096]{1,0:T(8,128)(2,1)S(1)} %get-tuple-element.28), channel_id=1, source_target_pairs={{0,1},{1,0},{2,3},{3,2},{4,5},{5,4},{6,7},{7,6},{8,9},{9,8},{10,11... | collective-permute-start | bytes 786440 | tf_op jit(solution)/shard_map/ppermute | solution.py:438
  57.9 7.5 %collective-permute-start.7 = (f32[8,128]{1,0:T(8,128)S(1)}, f32[8,128]{1,0:T(8,128)S(1)}, u32[]{:S(2)}, u32[]{:S(2)}) collective-permute-start(f32[8,128]{1,0:T(8,128)S(1)} %total.1.mine_ref), channel_id=1, source_target_pairs={{0,2},{2,0},{4,6},{6,4},{8,10},{10,8},{12,14},{14,12},{16,18},{18,... | collective-permute-start | bytes 12296 | tf_op jit(solution)/shard_map/ppermute | solution.py:441
  59.9 5.7 %copy-start.2 = (bf16[64,64,64]{2,1,0:T(8,128)(2,1)S(1)}, bf16[64,64,64]{2,1,0:T(8,128)(2,1)}, u32[]{:S(2)}) copy-start(bf16[64,64,64]{2,1,0:T(8,128)(2,1)} %basis_ref.1) | copy-start | bytes 1572868
  59.9 5.7 %copy-start.6 = (bf16[8192,128]{1,0:T(8,128)(2,1)S(1)}, bf16[8192,128]{1,0:T(8,128)(2,1)}, u32[]{:S(2)}) copy-start(bf16[8192,128]{1,0:T(8,128)(2,1)} %get-tuple-element.26.wide_ref) | copy-start | bytes 6291460
